TPU v7x, 32 devices: a whole 2x2x4 slice. The times are simulated.
32 devices in a mesh: groups: 2 (over y), ctx: 8 (over z, x), pb: 2 (over core).
Axes of the slice: x: 2, y: 2, z: 4, core: 2. Of those that a mesh axis runs over, the one named last changes fastest.
Arguments:
- att_query: bfloat16 [4, 8, 36864], P(('groups', 'pb'), 'ctx'), parts along dimension 0, may hold values from -26 to 26
- latent_cache: bfloat16 [4096, 576], P(('groups', 'ctx')), parts along dimension 0, may hold values from -6 to 6
- index_query: bfloat16 [4, 8, 4096], P(('groups', 'pb')), parts along dimension 0, may hold values from -70 to 70
- index_weight: float32 [4, 8, 32], P(('groups', 'pb')), parts along dimension 0, may hold values from -4 to 4
- index_keys: bfloat16 [4096, 128], P(('groups', 'ctx')), parts along dimension 0, may hold values from -16 to 16
- selected: int32 [4, 8, 1024], P(('groups', 'pb'), 'ctx'), parts along dimension 0, may hold values from 0 to 2047, as said below
Outputs:
- attended: bfloat16 [4, 8, 32768], P(('groups', 'pb'), 'ctx'), parts along dimension 0
- log_share: float32 [4, 8], P(('groups', 'pb')), parts along dimension 0
There are 2 independent parts, one for each index of `groups`. A program takes and returns all parts, laid end to end along the dimension named above; each array names one. Nothing has to cross between parts.
Inputs may be any that keep to these rules, and one draw needn't show every extreme that they name: `selected`: each query's 1024 positions are distinct, ascending, no later than its own position, and include its own position and the one before. In each query's list at most 256 positions fall in any aligned block of 256 keys, and in every draw some such block holds exactly 256 positions of every query.
All inputs are finite; a program needn't handle non-finite values.
Results may differ from a plain program's by a relative error of at most 0.01.
Values may be sent and summed in bfloat16 or wider, within the bound.
No kernel may reach another device: no remote copies, remote signals or barrier semaphores. Data moves between devices by JAX's collectives and lax.ppermute only.
A program may use at most 64 MiB of HBM per device.

v0:
```python
import jax
import jax.numpy as jnp
from jax import lax
from jax.sharding import PartitionSpec as P

HEADS = 64
LATENT = 512


score_scale = 192.0 ** (-0.5)
floor_value = -1e30


def combined_all(x, axis, combine):
    everything = jax.tree.map(lambda part: lax.all_gather(part, axis), x)
    initial = jax.tree.map(lambda part: part[0], everything)

    def turn(k, so_far):
        return combine(so_far, jax.tree.map(lambda part: part[k], everything))

    return lax.fori_loop(1, lax.axis_size(axis), turn, initial)


def merge_totals(left_part, right_part):
    peak_all = jnp.maximum(left_part[0], right_part[0])
    summed_all = left_part[1] * jnp.exp(left_part[0] - peak_all) + right_part[1] * jnp.exp(
        right_part[0] - peak_all
    )
    peak_sel = jnp.maximum(left_part[2], right_part[2])
    summed_sel = left_part[3] * jnp.exp(left_part[2] - peak_sel) + right_part[3] * jnp.exp(
        right_part[2] - peak_sel
    )
    return (peak_all, summed_all, peak_sel, summed_sel)


def masked_total(scores, keep_mask):
    highest = jnp.max(jnp.where(keep_mask, scores, floor_value), axis=1)
    summed = jnp.sum(jnp.where(keep_mask, jnp.exp(scores - highest[:, None]), 0.0), axis=1)
    return (highest, summed)


def index_scores(queries_here, weights_here, index_keys):
    row_count = weights_here.shape[0]
    head_count = weights_here.shape[1]
    key_count = index_keys.shape[0]
    width_here = index_keys.shape[1]
    block_size = min(512, key_count)
    stacked = queries_here.reshape(row_count * head_count, width_here)
    blocked = index_keys.reshape(key_count // block_size, block_size, width_here)

    def score_block(keys_block):
        products = lax.dot_general(
            stacked, keys_block, (((1,), (1,)), ((), ())), preferred_element_type=jnp.float32
        )
        rectified = jnp.maximum(products, 0.0).reshape(row_count, head_count, block_size)
        return jnp.sum(weights_here[:, :, None] * rectified, axis=1)

    pieces = lax.map(score_block, blocked)
    index_scale = float(head_count * width_here) ** (-0.5)
    return jnp.transpose(pieces, (1, 0, 2)).reshape(row_count, key_count) * index_scale


def attend_rows(queries_here, key_rows):
    scores = (
        jnp.einsum("qhd,qkd->qhk", queries_here, key_rows, preferred_element_type=jnp.float32)
        * score_scale
    )
    highest = jnp.max(scores, axis=2, keepdims=True)
    expo = jnp.exp(scores - highest)
    total = jnp.sum(expo, axis=2, keepdims=True)
    mixed = jnp.einsum(
        "qhk,qkd->qhd",
        expo.astype(jnp.bfloat16),
        key_rows[:, :, :LATENT],
        preferred_element_type=jnp.float32,
    )
    return (mixed / total).astype(jnp.bfloat16)


def body(att_query, latent_cache, index_query, index_weight, index_keys, selected):
    shards = lax.axis_size("ctx")
    shard_index = lax.axis_index("ctx")
    block_index = lax.axis_index("pb")
    block_total = lax.axis_size("pb")
    keys_here = latent_cache.shape[0]
    row_width = latent_cache.shape[1]
    per_block = index_query.shape[1]
    query_count = att_query.shape[1]
    top_count = selected.shape[2]
    capacity = 2 * top_count // shards
    keys_total = keys_here * shards
    query_total = per_block * block_total
    block_lists = lax.all_gather(selected, "ctx", axis=1, tiled=True)[0]
    query_places = keys_total - query_total + block_index * per_block + jnp.arange(per_block)
    key_places = shard_index * keys_here + jnp.arange(keys_here)
    scores = index_scores(index_query[0], index_weight[0], index_keys)
    causal = key_places[None, :] <= query_places[:, None]
    local_rows = block_lists - shard_index * keys_here
    inside = (local_rows >= 0) & (local_rows < keys_here)
    local_rows = jnp.where(inside, local_rows, keys_here)
    row_numbers = jnp.broadcast_to(jnp.arange(per_block)[:, None], local_rows.shape)
    chosen = (
        jnp.zeros((per_block, keys_here), jnp.bool_)
        .at[row_numbers, local_rows]
        .set(True, mode="drop")
    )
    peak_all, summed_all = masked_total(scores, causal)
    peak_sel, summed_sel = masked_total(scores, chosen)
    totals = combined_all((peak_all, summed_all, peak_sel, summed_sel), "ctx", merge_totals)
    log_share = totals[2] + jnp.log(totals[3]) - (totals[0] + jnp.log(totals[1]))
    own_lists = selected[0]
    owners = own_lists // keys_here
    offsets = own_lists - owners * keys_here
    owner_onehot = (owners[:, :, None] == jnp.arange(shards)[None, None, :]).astype(jnp.int32)
    counts = jnp.sum(owner_onehot, axis=1)
    starts = jnp.cumsum(counts, axis=1) - counts
    slots = jnp.arange(top_count)[None, :] - jnp.sum(owner_onehot * starts[:, None, :], axis=2)
    query_rows = jnp.broadcast_to(jnp.arange(query_count)[:, None], owners.shape)
    requests = (
        jnp.zeros((shards, query_count, capacity), jnp.int32)
        .at[owners, query_rows, slots]
        .set(offsets)
    )
    asked = lax.all_to_all(requests, "ctx", split_axis=0, concat_axis=0, tiled=True)
    picked = jnp.take(latent_cache, asked.reshape(-1), axis=0).reshape(asked.shape + (row_width,))
    fetched = lax.all_to_all(picked, "ctx", split_axis=0, concat_axis=0, tiled=True)
    flat_rows = fetched.reshape(shards * query_count * capacity, row_width)
    sources = (owners * query_count + query_rows) * capacity + slots
    gathered = jnp.take(flat_rows, sources.reshape(-1), axis=0).reshape(
        query_count, top_count, row_width
    )
    queries_mine = att_query[0].reshape(query_count, HEADS, row_width)
    attended = attend_rows(queries_mine, gathered)
    return (attended.reshape(1, query_count, HEADS * LATENT), log_share[None, :])


def solution(mesh):
    return jax.shard_map(
        body,
        mesh=mesh,
        in_specs=(
            P(("groups", "pb"), "ctx", None),
            P(("groups", "ctx"), None),
            P(("groups", "pb"), None, None),
            P(("groups", "pb"), None, None),
            P(("groups", "ctx"), None),
            P(("groups", "pb"), "ctx", None),
        ),
        out_specs=(P(("groups", "pb"), "ctx", None), P(("groups", "pb"), None)),
        check_vma=False,
    )
```

profile of v0, /device:TPU:0, one launch (start us, length us, event | category | flops | bytes accessed | tf_op | source)
XLA Modules:
  0.0 184.4 jit_solution(14206568549359155888)
XLA Ops:
  0.6 0.0 copy-start
  0.6 0.7 compare_select_fusion.4
  1.4 0.7 bitcast_subtract_fusion
  2.1 0.7 add_select_fusion
  2.8 0.1 convert_reduce_fusion
  2.9 0.2 reduce-window.7
  3.1 0.1 select_reduce_fusion
  3.2 0.7 and_reduce_fusion.1
  4.0 0.7 multiply_reduce_fusion.2
  4.7 4.9 %scatter_custom_fusion = s32[2048]{0:T(1024)} fusion(s32[1024]{0:T(1024)S(1)} %broadcast_select_fusion.1, s32[1024]{0:T(1024)S(1)} %bitcast.134, s32[]{:T(128)} %constant.113.clone.1), kind=kCustom, calls=%fused_computation.85 | custom fusion | bytes 8196
  9.6 7.3 %all-to-all-start = ((s32[8,1,256]{2,1,0:T(1,128)}), s32[8,1,256]{2,1,0:T(1,128)S(1)}, u32[]{:S(2)}, u32[]{:S(2)}) async-start(s32[8,1,256]{2,1,0:T(1,128)} %bitcast.11), calls=%async_computation | async-start | bytes 16384 | tf_op jit(solution)/shard_map/all_to_all | solution.py:124
  16.9 1.2 copy.14
  18.0 5.4 %all-to-all-done = s32[8,1,256]{2,1,0:T(1,128)S(1)} async-done(((s32[8,1,256]{2,1,0:T(1,128)}), s32[8,1,256]{2,1,0:T(1,128)S(1)}, u32[]{:S(2)}, u32[]{:S(2)}) %all-to-all-start) | async-done | bytes 8224 | tf_op jit(solution)/shard_map/all_to_all | solution.py:124
  23.4 7.7 %gather_fusion = bf16[2048,576]{1,0:T(8,128)(2,1)S(1)} fusion(bf16[256,576]{1,0:T(8,128)(2,1)S(1)} %copy.14, s32[2048]{0:T(1024)S(1)} %broadcast_clamp_fusion), kind=kCustom, calls=%fused_computation | custom fusion | bytes 4726784 | tf_op jit(solution)/shard_map/jit(_take)/gather | solution.py:125
  31.1 2.6 %copy.15 = bf16[8,1,256,576]{2,3,1,0:T(8,128)(2,1)} copy(bf16[8,1,256,576]{3,2,0,1:T(8,128)(2,1)S(1)} %bitcast.118) | data formatting | bytes 4718592 | tf_op jit(solution)/shard_map/jit(_take)/gather | solution.py:125
  33.7 3.3 %broadcast_select_fusion = bf16[8,1,256,576]{2,3,1,0:T(8,128)(2,1)} fusion(bf16[8,1,256,576]{2,3,1,0:T(8,128)(2,1)} %copy.15, pred[8,256]{1,0:T(8,128)(4,1)S(1)} %compare_and_fusion), kind=kLoop, calls=%fused_computation.18 | loop fusion | flops 1179648 | bytes 4720640 | tf_op jit(solution)/shard_map/jit(_take)/select_n | solution.py:125
  36.9 0.0 copy-start.4
  37.0 0.0 copy-start.8
  37.0 0.0 copy-start.5
  37.0 4.5 %all-to-all-start.1 = ((bf16[8,1,256,576]{2,3,1,0:T(8,128)(2,1)}), bf16[8,1,256,576]{2,3,1,0:T(8,128)(2,1)}, u32[]{:S(2)}, u32[]{:S(2)}) async-start(bf16[8,1,256,576]{2,3,1,0:T(8,128)(2,1)} %broadcast_select_fusion), calls=%async_computation.1 | async-start | bytes 4718592 | tf_op jit(solution)/shard_map/all_to_all | solution.py:126
  41.5 0.4 reduce.14
  41.9 0.1 reshape.742
  42.1 72.0 %all_gather.31 = s32[1,8,1024]{2,0,1:T(1,128)S(1)} all-gather(s32[1,1,1024]{2,0,1:T(1,128)S(1)} %bitcast.121), channel_id=1, replica_groups=mesh['groups'=2,'ctx'=8,'pb'=2] {'ctx'}, dimensions={1}, use_global_device_ids=true | all-gather | bytes 36864 | tf_op jit(solution)/shard_map/all_gather | solution.py:93
  114.0 0.1 compare_select_fusion
  114.1 0.1 multiply_reduce_fusion.1
  114.3 0.2 and_reduce_fusion
  114.5 34.6 %scatter_custom_fusion.1 = pred[2048]{0:T(1024)(128)(4,1)S(1)} fusion(s32[8192]{0:T(1024)S(1)} %bitcast.126, pred[8192]{0:T(1024)(128)(4,1)S(1)} %broadcast.590, pred[]{:T(512)} %constant.129.clone.1), kind=kCustom, calls=%fused_computation.89 | custom fusion | bytes 2049
  149.2 0.6 dynamic-slice.1
  150.5 0.2 multiply_reduce_fusion
  150.7 0.2 select_reduce_fusion.2
  150.9 0.2 dynamic-update-slice
  151.1 0.2 dynamic-update-slice.2
  151.3 0.2 select_reduce_fusion.1
  151.5 0.2 dynamic-update-slice.1
  151.8 0.2 dynamic-update-slice.3
  152.0 19.5 %all-reduce.4 = (f32[64]{0:T(128)S(1)}, f32[64]{0:T(128)S(1)}, f32[64]{0:T(128)S(1)}, f32[64]{0:T(128)S(1)}) all-reduce(f32[64]{0:T(128)S(1)} %dynamic-update-slice, f32[64]{0:T(128)S(1)} %dynamic-update-slice.1, f32[64]{0:T(128)S(1)} %dynamic-update-slice.2, f32[64]{0:T(128)S(1)} %dynamic-update-slice.3), channel_id=2, replica_groups=mesh['groups'=2,'ctx'=8,'pb'=2] {'ctx'}, use_global_device_ids=true, to_apply=%add | all-reduce | flops 256 | bytes 2048
  171.4 0.1 reshape.788
  171.5 0.1 reshape.789
  171.6 0.1 reshape.790
  171.7 0.1 reshape.791
  171.8 0.3 while.25
  172.1 0.5 subtract_bitcast_fusion
  172.7 3.1 %copy.16 = bf16[8,1,256,576]{3,2,0,1:T(8,128)(2,1)S(1)} copy(bf16[8,1,256,576]{2,3,1,0:T(8,128)(2,1)} %all-to-all-done.1) | data formatting | bytes 4718592 | tf_op jit(solution)/shard_map/all_to_all | solution.py:126
  175.8 5.1 %gather_fusion.1 = bf16[1024,576]{1,0:T(8,128)(2,1)} fusion(bf16[2048,576]{1,0:T(8,128)(2,1)S(1)} %bitcast.117, s32[1024]{0:T(1024)S(1)} %broadcast_clamp_fusion.1), kind=kCustom, calls=%fused_computation.1 | custom fusion | bytes 2363392 | tf_op jit(solution)/shard_map/jit(_take)/gather | solution.py:129
  181.0 2.1 %fusion.38 = (f32[64]{0:T(128)S(1)}, f32[1024,64]{0,1:T(8,128)S(1)}) fusion(bf16[64,576]{1,0:T(8,128)(2,1)S(1)} %reshape.742, bf16[1024,576]{1,0:T(8,128)(2,1)} %gather_fusion.1, pred[1024]{0:T(1024)(128)(4,1)S(1)} %compare_and_fusion.1), kind=kOutput, calls=%fused_computation.100 | convolution fusion | flops 76218304 | bytes 1516800 | tf_op jit(solution)/shard_map/qhd,qkd->qhk/dot_general | solution.py:65
  183.1 0.2 fusion.22
  183.3 0.4 fusion.16
  183.7 0.7 reshape.744
  (44 shorter events, 0.5 us)
Async XLA Ops:
  0.6 149.8 %copy-start = (bf16[256,128]{1,0:T(8,128)(2,1)S(1)}, bf16[256,128]{1,0:T(8,128)(2,1)}, u32[]{:S(2)}) copy-start(bf16[256,128]{1,0:T(8,128)(2,1)} %param.12) | copy-start | bytes 196612
  9.6 13.8 %all-to-all-start = ((s32[8,1,256]{2,1,0:T(1,128)}), s32[8,1,256]{2,1,0:T(1,128)S(1)}, u32[]{:S(2)}, u32[]{:S(2)}) async-start(s32[8,1,256]{2,1,0:T(1,128)} %bitcast.11), calls=%async_computation | async-start | bytes 16384 | tf_op jit(solution)/shard_map/all_to_all | solution.py:124
  36.9 4.6 %copy-start.3 = (bf16[1,1,36864]{2,1,0:T(2,128)(2,1)S(1)}, bf16[1,1,36864]{2,1,0:T(2,128)(2,1)}, u32[]{:S(2)}) copy-start(bf16[1,1,36864]{2,1,0:T(2,128)(2,1)} %param.8) | copy-start | bytes 221188
  36.9 5.1 %copy-start.2 = (s32[1,1,1024]{2,1,0:T(1,128)S(1)}, s32[1,1,1024]{2,1,0:T(1,128)}, u32[]{:S(2)}) copy-start(s32[1,1,1024]{2,1,0:T(1,128)} %param.13) | copy-start | bytes 12292
  36.9 77.2 %copy-start.7 = (s32[2]{0:T(128)S(1)}, s32[2]{0:T(128)}, u32[]{:S(2)}) copy-start(s32[2]{0:T(128)} %constant.141) | copy-start | bytes 28
  36.9 77.4 %copy-start.6 = (s32[2]{0:T(128)S(1)}, s32[2]{0:T(128)}, u32[]{:S(2)}) copy-start(s32[2]{0:T(128)} %constant.144) | copy-start | bytes 28
  36.9 112.2 %copy-start.4 = (bf16[1,8,4096]{2,1,0:T(8,128)(2,1)S(1)}, bf16[1,8,4096]{2,1,0:T(8,128)(2,1)}, u32[]{:S(2)}) copy-start(bf16[1,8,4096]{2,1,0:T(8,128)(2,1)} %param.10) | copy-start | bytes 196612
  37.0 112.2 %copy-start.8 = (u32[32]{0:T(128)S(1)}, u32[32]{0:T(128)}, u32[]{:S(2)}) copy-start(u32[32]{0:T(128)} %constant.152) | copy-start | bytes 388
  37.0 113.5 %copy-start.5 = (f32[1,8,32]{2,1,0:T(8,128)S(1)}, f32[1,8,32]{2,1,0:T(8,128)}, u32[]{:S(2)}) copy-start(f32[1,8,32]{2,1,0:T(8,128)} %param.11) | copy-start | bytes 3076
  37.0 135.7 %all-to-all-start.1 = ((bf16[8,1,256,576]{2,3,1,0:T(8,128)(2,1)}), bf16[8,1,256,576]{2,3,1,0:T(8,128)(2,1)}, u32[]{:S(2)}, u32[]{:S(2)}) async-start(bf16[8,1,256,576]{2,3,1,0:T(8,128)(2,1)} %broadcast_select_fusion), calls=%async_computation.1 | async-start | bytes 4718592 | tf_op jit(solution)/shard_map/all_to_all | solution.py:126
  181.0 2.4 %copy-start.1 = (bf16[1024,576]{1,0:T(8,128)(2,1)S(1)}, bf16[1024,576]{1,0:T(8,128)(2,1)}, u32[]{:S(2)}) copy-start(bf16[1024,576]{1,0:T(8,128)(2,1)} %gather_fusion.1) | copy-start | bytes 3538948
where the time goes:
time: 185 us; the launch traced here: 184 us
  blocking collectives  91.4 us (49%)
  local copies, waits for them, and re-layouts  61.8 us (33%)
  starting transfers between devices  11.8 us (6%)
  other arithmetic  9.57 us (5%)
  waiting for transfers between devices  5.36 us (3%)
  matrix products  2.7 us (1%)
    all_gather x1, blocking collectives, body(): block_lists = lax.all_gather(selected, 'ctx', axis=1, tiled=True)[0]  72 us
    unnamed x32, local copies, waits for them, and re-layouts  42.2 us
    unnamed x1, blocking collectives  19.5 us
    gather x2, local copies, waits for them, and re-layouts, body(): jnp.take(latent_cache, asked.reshape(-1), axis=0)  10.2 us
    all_to_all x1, starting transfers between devices, body(): lax.all_to_all(requests, 'ctx', split_axis=0, concat_axis=0, tiled=True)  7.25 us
    all_to_all x1, waiting for transfers between devices, body(): lax.all_to_all(requests, 'ctx', split_axis=0, concat_axis=0, tiled=True)  5.35 us
    gather x1, local copies, waits for them, and re-layouts, body(): jnp.take(flat_rows, sources.reshape(-1), axis=0)  5.15 us
    all_to_all x1, starting transfers between devices, body(): lax.all_to_all(picked, 'ctx', split_axis=0, concat_axis=0, tiled=True)  4.51 us
  transfers between devices with their start and end apart: 2, of which 1 were waited for; matrix products, arithmetic and copies ran while one was open for 22% of the time, Pallas kernels for 0%

commit v1 on v0

v1 whole, which is shorter than its diff:
```python
import functools

import jax
import jax.numpy as jnp
from jax import lax
from jax.experimental import pallas as pl
from jax.experimental.pallas import tpu as pltpu
from jax.sharding import PartitionSpec as P

HEADS = 64
LATENT = 512
LANES = 128
SPAN = 4

score_scale = 192.0 ** (-0.5)
floor_value = -1e30

NT = (((1,), (1,)), ((), ()))
NN = (((1,), (0,)), ((), ()))


def round_up(count, step):
    return -(-count // step) * step


def swap(x, offset):
    size = lax.axis_size("ctx")
    return lax.ppermute(x, "ctx", [(i, i ^ offset) for i in range(size)])


def swap_cores(x):
    size = lax.axis_size("pb")
    return lax.ppermute(x, "pb", [(i, i ^ 1) for i in range(size)])


def swap_apart(x, even_offset, odd_offset):
    size, cores = lax.axis_size("ctx"), lax.axis_size("pb")
    moves = []
    for i in range(size):
        for c in range(cores):
            partner = i ^ (odd_offset if c % 2 else even_offset)
            moves.append((i * cores + c, partner * cores + c))
    return lax.ppermute(x, ("ctx", "pb"), moves)


def call(kernel, out_shape, scratch=(), **kwargs):
    return pl.pallas_call(
        kernel,
        out_shape=out_shape,
        scratch_shapes=list(scratch),
        compiler_params=pltpu.CompilerParams(vmem_limit_bytes=40 * 2**20),
        **kwargs,
    )


def prepare_kernel(query_ref, index_query_ref, weight_ref, keys_ref, list_ref, packed_ref, share_ref):
    keys_here, width = keys_ref.shape
    rows, head_count = weight_ref.shape
    shards = share_ref.shape[0] - rows
    top_count = list_ref.shape[1]
    row_width = query_ref.shape[1]
    places = list_ref[...]
    low = places % LANES
    high = places // LANES
    low_hot = (lax.broadcasted_iota(jnp.int32, (LANES, top_count), 0) == low).astype(jnp.bfloat16)
    part_count = keys_here // LANES
    owner = lax.broadcasted_iota(jnp.int32, (shards, top_count), 0) * part_count
    parts = []
    for part in range(part_count):
        high_hot = (owner + part == high).astype(jnp.bfloat16)
        parts.append(lax.dot_general(high_hot, low_hot, NT, preferred_element_type=jnp.float32))
    mask = jnp.concatenate(parts, axis=1)
    pad_rows = packed_ref.shape[0] - HEADS - shards
    wide = jnp.concatenate([mask, jnp.zeros((shards, row_width - keys_here), jnp.float32)], axis=1)
    if pad_rows:
        wide = jnp.concatenate([wide, jnp.zeros((pad_rows, row_width), jnp.float32)], axis=0)
    packed_ref[HEADS:, :] = wide.astype(jnp.bfloat16)
    packed_ref[:HEADS, :] = query_ref[...]
    stacked = jnp.concatenate(
        [index_query_ref[:, h * width : (h + 1) * width].astype(jnp.float32) for h in range(head_count)], axis=0
    ).astype(jnp.bfloat16)
    products = lax.dot_general(stacked, keys_ref[...], NT, preferred_element_type=jnp.float32)
    total = jnp.zeros((rows, keys_here), jnp.float32)
    for h in range(head_count):
        total += weight_ref[:, h : h + 1] * jnp.maximum(products[h * rows : (h + 1) * rows], 0.0)
    share_ref[:rows, :] = total * float(head_count * width) ** (-0.5)
    share_ref[rows:, :] = mask


def attend(packed_ref, row_refs, far_ref, mask_ref):
    me = lax.axis_index("ctx")
    odd = lax.axis_index("pb") % 2
    keys_here = row_refs[0].shape[1]
    owners = [me, me ^ (1 + odd), me ^ (2 - odd), me ^ 3]
    mask_ref[...] = packed_ref[HEADS:, :keys_here].astype(jnp.float32)
    queries = packed_ref[:HEADS, :]
    refs = list(row_refs) + [far_ref]
    pieces = []
    for owner, ref in zip(owners, refs):
        piece = lax.dot_general(queries, ref[...], NN, preferred_element_type=jnp.float32) * score_scale
        keep = mask_ref[pl.ds(owner, 1), :] > 0.5
        pieces.append(jnp.where(keep, piece, floor_value))
    scores = jnp.concatenate(pieces, axis=1)
    highest = jnp.max(scores, axis=1, keepdims=True)
    expo = jnp.where(scores > 0.5 * floor_value, jnp.exp(scores - highest), 0.0)
    total = jnp.sum(expo, axis=1, keepdims=True)
    rounded = expo.astype(jnp.bfloat16)
    mixed = jnp.zeros((HEADS, LATENT), jnp.float32)
    for j, ref in enumerate(refs):
        mixed += lax.dot_general(
            rounded[:, j * keys_here : (j + 1) * keys_here], ref[:LATENT, :], NT, preferred_element_type=jnp.float32
        )
    some = total > 0.0
    safe = jnp.where(some, total, 1.0)
    return mixed / safe, jnp.where(some, highest + jnp.log(safe), floor_value)


def fill_far(half_ref, other_ref, far_ref):
    odd = lax.axis_index("pb") % 2
    rows = half_ref.shape[0]
    far_ref[pl.ds(pl.multiple_of(odd * rows, 16), rows), :] = half_ref[...]
    far_ref[pl.ds(pl.multiple_of((1 - odd) * rows, 16), rows), :] = other_ref[...]


def send_kernel(packed_ref, own_ref, first_ref, second_ref, half_ref, other_ref, out_ref, far_ref, mask_ref):
    fill_far(half_ref, other_ref, far_ref)
    mixed, lse = attend(packed_ref, (own_ref, first_ref, second_ref), far_ref, mask_ref)
    high = lse.astype(jnp.bfloat16)
    rest = lse - high.astype(jnp.float32)
    middle = rest.astype(jnp.bfloat16)
    last = (rest - middle.astype(jnp.float32)).astype(jnp.bfloat16)
    lane = lax.broadcasted_iota(jnp.int32, (HEADS, LANES), 1)
    tail = jnp.where(
        lane == 0,
        high.astype(jnp.float32),
        jnp.where(lane == 1, middle.astype(jnp.float32), last.astype(jnp.float32)),
    )
    out_ref[:, :LATENT] = mixed.astype(jnp.bfloat16)
    out_ref[:, LATENT:] = tail.astype(jnp.bfloat16)


def keep_kernel(packed_ref, own_ref, first_ref, second_ref, half_ref, other_ref, out_ref, lse_ref, far_ref, mask_ref):
    fill_far(half_ref, other_ref, far_ref)
    mixed, lse = attend(packed_ref, (own_ref, first_ref, second_ref), far_ref, mask_ref)
    out_ref[...] = mixed
    lse_ref[...] = jnp.broadcast_to(lse, lse_ref.shape)


def combine_kernel(own_ref, lse_ref, *refs):
    out_ref = refs[-1]
    mixes, lses = [own_ref[...]], [lse_ref[:, :1]]
    for ref in refs[:-1]:
        tail = ref[:, LATENT:].astype(jnp.float32)
        lses.append(tail[:, 0:1] + tail[:, 1:2] + tail[:, 2:3])
        mixes.append(ref[:, :LATENT].astype(jnp.float32))
    peak = functools.reduce(jnp.maximum, lses)
    weights = [jnp.exp(lse - peak) for lse in lses]
    total = functools.reduce(jnp.add, weights)
    mixed = functools.reduce(jnp.add, [w * m for w, m in zip(weights, mixes)])
    out_ref[...] = (mixed / total).astype(jnp.bfloat16)


def share_kernel(offsets, first_place, *refs):
    *block_refs, out_ref, scores_ref, mask_ref = refs
    shards, rows, keys_here = scores_ref.shape
    me = lax.axis_index("ctx")
    k = 0
    for ref in block_refs:
        for j in range(ref.shape[0]):
            owner = me ^ offsets[k]
            scores_ref[owner] = ref[j, :rows, :]
            mask_ref[owner] = ref[j, rows:, :]
            k += 1
    start = first_place + lax.axis_index("pb") * rows
    query_place = start + lax.broadcasted_iota(jnp.int32, (rows, keys_here), 0)
    key_place = lax.broadcasted_iota(jnp.int32, (rows, keys_here), 1)
    causal = [key_place + t * keys_here <= query_place for t in range(shards)]
    chosen = [mask_ref[:, t, :] > 0.5 for t in range(shards)]

    def lse(keeps):
        peak = jnp.full((rows, keys_here), floor_value, jnp.float32)
        for t in range(shards):
            peak = jnp.maximum(peak, jnp.where(keeps[t], scores_ref[t], floor_value))
        peak = jnp.max(peak, axis=1, keepdims=True)
        total = jnp.zeros((rows, keys_here), jnp.float32)
        for t in range(shards):
            total += jnp.where(keeps[t], jnp.exp(scores_ref[t] - peak), 0.0)
        return peak + jnp.log(jnp.sum(total, axis=1, keepdims=True))

    share = lse(chosen) - lse(causal)
    diagonal = lax.broadcasted_iota(jnp.int32, (rows, rows), 0) == lax.broadcasted_iota(jnp.int32, (rows, rows), 1)
    out_ref[...] = jnp.sum(jnp.where(diagonal, share, 0.0), axis=0, keepdims=True)


def body(att_query, latent_cache, index_query, index_weight, index_keys, selected):
    shards = lax.axis_size("ctx")
    blocks = lax.axis_size("pb")
    keys_here, row_width = latent_cache.shape
    rows = index_query.shape[1]
    bf16, f32 = jnp.bfloat16, jnp.float32
    shape = jax.ShapeDtypeStruct

    latent = latent_cache.T
    near = swap_apart(latent, 1, 2)
    half_rows = row_width // 2
    half = lax.dynamic_slice_in_dim(latent, (lax.axis_index("pb") % 2) * half_rows, half_rows, 0)
    far_half = swap(half, 3)

    packed_rows = HEADS + round_up(shards, 16)
    packed, share_own = call(
        prepare_kernel,
        (shape((packed_rows, row_width), bf16), shape((rows + shards, keys_here), f32)),
    )(att_query.reshape(HEADS, row_width), index_query[0], index_weight[0], index_keys, selected[0])

    near_other = swap_cores(near)
    far_other = swap_cores(far_half)
    span_rows = (latent, near, near_other, far_half, far_other)

    scratch = (pltpu.VMEM((row_width, keys_here), bf16), pltpu.VMEM((packed_rows - HEADS, keys_here), f32))
    parts = []
    for k in range(1, shards // SPAN):
        asked = swap(packed, SPAN * k)
        part = call(send_kernel, shape((HEADS, LATENT + LANES), bf16), scratch)(asked, *span_rows)
        parts.append(swap(part, SPAN * k))
    kept, kept_lse = call(
        keep_kernel, (shape((HEADS, LATENT), f32), shape((HEADS, LANES), f32)), scratch
    )(packed, *span_rows)
    attended = call(combine_kernel, shape((HEADS, LATENT), bf16))(kept, kept_lse, *parts)

    held, offsets = share_own[None], [0]
    bits = [1 << b for b in range(shards.bit_length() - 1)]
    arrived = held
    for bit in bits:
        if bit != bits[0]:
            held = jnp.concatenate([held, arrived], axis=0)
        arrived = swap(held, bit)
        offsets = offsets + [o ^ bit for o in offsets]
    log_share = call(
        functools.partial(share_kernel, offsets, keys_here * shards - rows * blocks),
        shape((1, rows), f32),
        (pltpu.VMEM((shards, rows, keys_here), f32), pltpu.VMEM((shards, shards, keys_here), f32)),
    )(held, arrived)
    return attended.reshape(1, 1, HEADS * LATENT), log_share


def solution(mesh):
    return jax.shard_map(
        body,
        mesh=mesh,
        in_specs=(
            P(("groups", "pb"), "ctx", None),
            P(("groups", "ctx"), None),
            P(("groups", "pb"), None, None),
            P(("groups", "pb"), None, None),
            P(("groups", "ctx"), None),
            P(("groups", "pb"), "ctx", None),
        ),
        out_specs=(P(("groups", "pb"), "ctx", None), P(("groups", "pb"), None)),
        check_vma=False,
    )
```

time: 185 us -> 36.7 us (0.20)
  blocking collectives: 91.4 us -> 0 us
  local copies, waits for them, and re-layouts: 61.8 us -> 2.5 us
  waiting for transfers between devices: 5.36 us -> 15.4 us
  other arithmetic: 9.57 us -> 0.43 us
  Pallas kernels: 0 us -> 2.93 us
  matrix products: 2.7 us -> 0 us
  starting transfers between devices: 11.8 us -> 14.5 us
    all_gather x1 -> x0, blocking collectives: 72 us -> none  [body(): block_lists = lax.all_gather(selected, 'ctx', axis=1, tiled=True)[0]]
    unnamed x32 -> x12, local copies, waits for them, and re-layouts: 42.2 us -> 0.71 us
    unnamed x1 -> x0, blocking collectives: 19.5 us -> none
    ppermute x0 -> x9, waiting for transfers between devices: none -> 15.4 us  [the longest x6 10.3 us: swap(): return lax.ppermute(x, 'ctx', [(i, i ^ offset) for i in range(size)])]
    gather x3 -> x0, local copies, waits for them, and re-layouts: 15.4 us -> none  [the longest x2 10.2 us: body(): jnp.take(latent_cache, asked.reshape(-1), axis=0)]
    ppermute x0 -> x9, starting transfers between devices: none -> 14.5 us  [the longest x6 11.3 us: swap(): return lax.ppermute(x, 'ctx', [(i, i ^ offset) for i in range(size)])]
    all_to_all x2 -> x0, starting transfers between devices: 11.8 us -> none  [the longest x1 7.25 us: body(): lax.all_to_all(requests, 'ctx', split_axis=0, concat_axis=0, tiled=True)]
    all_to_all x2 -> x0, waiting for transfers between devices: 5.36 us -> none  [the longest x1 5.35 us: body(): lax.all_to_all(requests, 'ctx', split_axis=0, concat_axis=0, tiled=True)]
  transfers between devices with their start and end apart: 2 -> 9, of which waited for: 1 -> 3; matrix products, arithmetic and copies ran while one was open for 22% -> 4% of each run, Pallas kernels for 0% -> 8%
where the time goes in v1:
time: 36.7 us; the launch traced here: 36.5 us
  waiting for transfers between devices  15.4 us (42%)
  starting transfers between devices  14.5 us (40%)
  Pallas kernels  2.93 us (8%)
  local copies, waits for them, and re-layouts  2.5 us (7%)
  between operations  0.72 us (2%)
  other arithmetic  0.43 us (1%)
    ppermute x6, starting transfers between devices, swap(): return lax.ppermute(x, 'ctx', [(i, i ^ offset) for i in range(size)])  11.3 us
    ppermute x6, waiting for transfers between devices, swap(): return lax.ppermute(x, 'ctx', [(i, i ^ offset) for i in range(size)])  10.3 us
    ppermute x1, waiting for transfers between devices, swap_apart(): return lax.ppermute(x, ('ctx', 'pb'), moves)  5.1 us
    ppermute x1, starting transfers between devices, swap_apart(): return lax.ppermute(x, ('ctx', 'pb'), moves)  3 us
    dynamic_slice x1, local copies, waits for them, and re-layouts, body(): lax.dynamic_slice_in_dim(latent, lax.axis_index('pb') % 2 * half_rows, ha...  0.99 us
    pallas_call x1, Pallas kernels, body(): call(keep_kernel, (shape((HEADS, LATENT), f32), shape((HEADS, LANES), f32...  0.8 us
    pallas_call x1, Pallas kernels, body(): call(send_kernel, shape((HEADS, LATENT + LANES), bf16), scratch)  0.8 us
    pallas_call x1, Pallas kernels, body(): call(functools.partial(share_kernel, offsets, keys_here * shards - rows *...  0.78 us
  transfers between devices with their start and end apart: 9, of which 3 were waited for; matrix products, arithmetic and copies ran while one was open for 4% of the time, Pallas kernels for 8%

profile of v1, /device:TPU:0, one launch (start us, length us, event | category | flops | bytes accessed | tf_op | source)
XLA Modules:
  0.0 36.5 jit_solution(18423296916765371671)
XLA Ops:
  0.6 3.0 %collective-permute-start = (bf16[576,256]{1,0:T(8,128)(2,1)}, bf16[576,256]{1,0:T(8,128)(2,1)S(1)}, u32[]{:S(2)}, u32[]{:S(2)}) collective-permute-start(bf16[576,256]{1,0:T(8,128)(2,1)} %bitcast.7), channel_id=1, source_target_pairs={{0,2},{1,5},{2,0},{3,7},{4,6},{5,1},{6,4},{7,3},{8,10},{9,13},{10,... | collective-permute-start | bytes 884744 | tf_op jit(solution)/shard_map/ppermute | solution.py:43
  3.6 0.0 copy-start.5
  3.6 0.0 copy-start.2
  3.6 1.0 %dynamic-slice_bitcast_fusion = bf16[288,256]{1,0:T(8,128)(2,1)S(1)} fusion(bf16[256,576]{0,1:T(8,128)(2,1)} %param.7, s32[]{:T(128)S(6)} %select_n.11), kind=kLoop, calls=%fused_computation | loop fusion | bytes 294916 | tf_op jit(solution)/shard_map/dynamic_slice | solution.py:206
  4.6 0.0 copy-start
  4.6 1.6 %collective-permute-start.2 = (bf16[288,256]{1,0:T(8,128)(2,1)S(1)}, bf16[288,256]{1,0:T(8,128)(2,1)S(1)}, u32[]{:S(2)}, u32[]{:S(2)}) collective-permute-start(bf16[288,256]{1,0:T(8,128)(2,1)S(1)} %dynamic-slice_bitcast_fusion), channel_id=1, source_target_pairs={{0,6},{2,4},{4,2},{6,0},{8,14},{10,12},{12,10},{14,8},{1,7},{3,5},... | collective-permute-start | bytes 442376 | tf_op jit(solution)/shard_map/ppermute | solution.py:28
  6.3 5.1 %collective-permute-done.first_ref = bf16[576,256]{1,0:T(8,128)(2,1)S(1)} collective-permute-done((bf16[576,256]{1,0:T(8,128)(2,1)}, bf16[576,256]{1,0:T(8,128)(2,1)S(1)}, u32[]{:S(2)}, u32[]{:S(2)}) %collective-permute-start) | collective-permute-done | bytes 294944 | tf_op jit(solution)/shard_map/ppermute | solution.py:43
  11.4 0.0 collective-permute-start.1
  11.4 0.0 copy-done.5
  11.4 0.4 %reduce = bf16[36864]{0:T(1024)(128)(2,1)S(1)} reduce(bf16[1,1,36864]{2,1,0:T(2,128)(2,1)S(1)} %copy-done.5, bf16[]{:T(256)} %constant.26), dimensions={0,1}, to_apply=%param.6.reduce_sub_computation | reduce | bytes 147458 | tf_op args[0]
  11.8 0.0 copy-start.1
  11.8 0.0 copy-start.4
  11.8 0.1 reshape.10.query_ref
  11.9 0.0 copy-start.3
  11.9 0.0 copy-done.2
  11.9 0.7 %copy-done.1 = bf16[1,8,4096]{2,1,0:T(8,128)(2,1)S(1)} copy-done((bf16[1,8,4096]{2,1,0:T(8,128)(2,1)S(1)}, bf16[1,8,4096]{2,1,0:T(8,128)(2,1)}, u32[]{:S(2)}) %copy-start.1) | copy-done | bytes 65560
  12.6 0.0 copy-done.4
  12.6 0.0 copy-done.3
  12.6 0.4 shard_map.77
  13.0 2.4 %collective-permute-start.6 = (f32[1,16,256]{2,1,0:T(8,128)S(1)}, f32[1,16,256]{2,1,0:T(8,128)S(1)}, u32[]{:S(2)}, u32[]{:S(2)}) collective-permute-start(f32[1,16,256]{2,1,0:T(8,128)S(1)} %bitcast.11), channel_id=1, source_target_pairs={{0,2},{2,0},{4,6},{6,4},{8,10},{10,8},{12,14},{14,12},{1,3},{3,1},... | collective-permute-start | bytes 49160 | tf_op jit(solution)/shard_map/ppermute | solution.py:28
  15.4 0.0 collective-permute-done.2.half_ref
  15.4 0.2 collective-permute-start.3
  15.7 2.6 %collective-permute-start.4 = (bf16[80,576]{1,0:T(8,128)(2,1)S(1)}, bf16[80,576]{1,0:T(8,128)(2,1)S(1)}, u32[]{:S(2)}, u32[]{:S(2)}) collective-permute-start(bf16[80,576]{1,0:T(8,128)(2,1)S(1)} %get-tuple-element.6.packed_ref), channel_id=1, source_target_pairs={{0,8},{2,10},{4,12},{6,14},{8,0},{10,2},{12,4},{14,6},{1,9},{3,11}... | collective-permute-start | bytes 276488 | tf_op jit(solution)/shard_map/ppermute | solution.py:28
  18.3 0.0 collective-permute-done.6
  18.3 1.6 %collective-permute-start.7 = (f32[2,16,256]{2,1,0:T(8,128)S(1)}, f32[2,16,256]{2,1,0:T(8,128)S(1)}, u32[]{:S(2)}, u32[]{:S(2)}) collective-permute-start(f32[2,16,256]{2,1,0:T(8,128)S(1)} %pad_maximum_fusion.1), channel_id=1, source_target_pairs={{0,4},{2,6},{4,0},{6,2},{8,12},{10,14},{12,8},{14,10},{1,5},{3,7},... | collective-permute-start | bytes 98312 | tf_op jit(solution)/shard_map/ppermute | solution.py:28
  19.8 4.0 %collective-permute-done.4.packed_ref = bf16[80,576]{1,0:T(8,128)(2,1)S(1)} collective-permute-done((bf16[80,576]{1,0:T(8,128)(2,1)S(1)}, bf16[80,576]{1,0:T(8,128)(2,1)S(1)}, u32[]{:S(2)}, u32[]{:S(2)}) %collective-permute-start.4) | collective-permute-done | bytes 92192 | tf_op jit(solution)/shard_map/ppermute | solution.py:28
  23.8 0.0 collective-permute-done.3.other_ref
  23.8 0.0 collective-permute-done.1.second_ref
  23.8 0.0 copy-done
  23.8 0.8 %shard_map.79 = bf16[64,640]{1,0:T(8,128)(2,1)S(1)} custom-call(bf16[80,576]{1,0:T(8,128)(2,1)S(1)} %collective-permute-done.4.packed_ref, bf16[576,256]{1,0:T(8,128)(2,1)S(1)} %bitcast.8, bf16[576,256]{1,0:T(8,128)(2,1)S(1)} %collective-permute-done.first_ref, bf16[576,256]{1,0:T(8,128)(2,1)S(1)} %collective-permute-done.1.second_ref, ...), custom_call_target="tpu_custom_call" | custom-call | tf_op jit(solution)/shard_map/pallas_call | solution.py:223
  24.6 0.8 %collective-permute-start.5 = (bf16[64,640]{1,0:T(8,128)(2,1)S(1)}, bf16[64,640]{1,0:T(8,128)(2,1)S(1)}, u32[]{:S(2)}, u32[]{:S(2)}) collective-permute-start(bf16[64,640]{1,0:T(8,128)(2,1)S(1)} %shard_map.79), channel_id=1, source_target_pairs={{0,8},{2,10},{4,12},{6,14},{8,0},{10,2},{12,4},{14,6},{1,9},{3,11}... | collective-permute-start | bytes 245768 | tf_op jit(solution)/shard_map/ppermute | solution.py:28
  25.5 0.0 collective-permute-done.7
  25.5 2.2 %collective-permute-start.8 = (f32[4,16,256]{2,1,0:T(8,128)S(1)}, f32[4,16,256]{2,1,0:T(8,128)S(1)}, u32[]{:S(2)}, u32[]{:S(2)}) collective-permute-start(f32[4,16,256]{2,1,0:T(8,128)S(1)} %pad_maximum_fusion.refs_0_), channel_id=1, source_target_pairs={{0,8},{2,10},{4,12},{6,14},{8,0},{10,2},{12,4},{14,6},{1,9},{3,11}... | collective-permute-start | bytes 196616 | tf_op jit(solution)/shard_map/ppermute | solution.py:28
  27.7 6.3 %collective-permute-done.8.refs_1_ = f32[4,16,256]{2,1,0:T(8,128)S(1)} collective-permute-done((f32[4,16,256]{2,1,0:T(8,128)S(1)}, f32[4,16,256]{2,1,0:T(8,128)S(1)}, u32[]{:S(2)}, u32[]{:S(2)}) %collective-permute-start.8) | collective-permute-done | bytes 65568 | tf_op jit(solution)/shard_map/ppermute | solution.py:28
  34.0 0.8 %shard_map.81 = f32[1,8]{1,0:T(1,128)} custom-call(f32[4,16,256]{2,1,0:T(8,128)S(1)} %pad_maximum_fusion.refs_0_, f32[4,16,256]{2,1,0:T(8,128)S(1)} %collective-permute-done.8.refs_1_), custom_call_target="tpu_custom_call" | custom-call | tf_op jit(solution)/shard_map/pallas_call | solution.py:238
  34.8 0.8 %shard_map.78 = (f32[64,512]{1,0:T(8,128)S(1)}, f32[64,128]{1,0:T(8,128)S(1)}) custom-call(bf16[80,576]{1,0:T(8,128)(2,1)S(1)} %get-tuple-element.6.packed_ref, bf16[576,256]{1,0:T(8,128)(2,1)S(1)} %bitcast.9, bf16[576,256]{1,0:T(8,128)(2,1)S(1)} %collective-permute-done.first_ref, bf16[576,256]{1,0:T(8,128)(2,1)S(1)} %collective-permute-done.1.second_ref, ...), custom_call_target="tpu_custom_call" | custom-call | tf_op jit(solution)/shard_map/pallas_call | solution.py:225
  35.6 0.0 collective-permute-done.5.refs_0_
  35.6 0.2 shard_map.80
  35.8 0.7 %reshape.11 = bf16[1,1,32768]{2,1,0:T(2,128)(2,1)} reshape(bf16[64,512]{1,0:T(8,128)(2,1)S(1)} %shard_map.80) | data formatting | bytes 131072 | tf_op jit(solution)/shard_map/reshape | solution.py:243
  (2 shorter events, 0.0 us)
Async XLA Ops:
  0.6 10.7 %collective-permute-start = (bf16[576,256]{1,0:T(8,128)(2,1)}, bf16[576,256]{1,0:T(8,128)(2,1)S(1)}, u32[]{:S(2)}, u32[]{:S(2)}) collective-permute-start(bf16[576,256]{1,0:T(8,128)(2,1)} %bitcast.7), channel_id=1, source_target_pairs={{0,2},{1,5},{2,0},{3,7},{4,6},{5,1},{6,4},{7,3},{8,10},{9,13},{10,... | collective-permute-start | bytes 884744 | tf_op jit(solution)/shard_map/ppermute | solution.py:43
  3.6 7.7 %copy-start.5 = (bf16[1,1,36864]{2,1,0:T(2,128)(2,1)S(1)}, bf16[1,1,36864]{2,1,0:T(2,128)(2,1)}, u32[]{:S(2)}) copy-start(bf16[1,1,36864]{2,1,0:T(2,128)(2,1)} %param.6) | copy-start | bytes 221188
  3.6 8.3 %copy-start.2 = (bf16[256,128]{1,0:T(8,128)(2,1)S(1)}, bf16[256,128]{1,0:T(8,128)(2,1)}, u32[]{:S(2)}) copy-start(bf16[256,128]{1,0:T(8,128)(2,1)} %keys_ref.1) | copy-start | bytes 196612
  4.6 19.2 %copy-start = (bf16[256,576]{0,1:T(8,128)(2,1)S(1)}, bf16[256,576]{0,1:T(8,128)(2,1)}, u32[]{:S(2)}) copy-start(bf16[256,576]{0,1:T(8,128)(2,1)} %param.7) | copy-start | bytes 884740
  4.6 10.8 %collective-permute-start.2 = (bf16[288,256]{1,0:T(8,128)(2,1)S(1)}, bf16[288,256]{1,0:T(8,128)(2,1)S(1)}, u32[]{:S(2)}, u32[]{:S(2)}) collective-permute-start(bf16[288,256]{1,0:T(8,128)(2,1)S(1)} %dynamic-slice_bitcast_fusion), channel_id=1, source_target_pairs={{0,6},{2,4},{4,2},{6,0},{8,14},{10,12},{12,10},{14,8},{1,7},{3,5},... | collective-permute-start | bytes 442376 | tf_op jit(solution)/shard_map/ppermute | solution.py:28
  11.4 12.5 %collective-permute-start.1 = (bf16[576,256]{1,0:T(8,128)(2,1)S(1)}, bf16[576,256]{1,0:T(8,128)(2,1)S(1)}, u32[]{:S(2)}, u32[]{:S(2)}) collective-permute-start(bf16[576,256]{1,0:T(8,128)(2,1)S(1)} %collective-permute-done.first_ref), channel_id=1, source_target_pairs={{0,1},{1,0},{2,3},{3,2},{4,5},{5,4},{6,7},{7,6},{8,9},{9,8},{10,11... | collective-permute-start | bytes 884744 | tf_op jit(solution)/shard_map/ppermute | solution.py:33
  11.8 0.8 %copy-start.1 = (bf16[1,8,4096]{2,1,0:T(8,128)(2,1)S(1)}, bf16[1,8,4096]{2,1,0:T(8,128)(2,1)}, u32[]{:S(2)}) copy-start(bf16[1,8,4096]{2,1,0:T(8,128)(2,1)} %param.8) | copy-start | bytes 196612
  11.8 0.8 %copy-start.4 = (s32[1,1,1024]{2,1,0:T(1,128)S(1)}, s32[1,1,1024]{2,1,0:T(1,128)}, u32[]{:S(2)}) copy-start(s32[1,1,1024]{2,1,0:T(1,128)} %param.11) | copy-start | bytes 12292
  11.9 0.7 %copy-start.3 = (f32[1,8,32]{2,1,0:T(8,128)S(1)}, f32[1,8,32]{2,1,0:T(8,128)}, u32[]{:S(2)}) copy-start(f32[1,8,32]{2,1,0:T(8,128)} %param.9) | copy-start | bytes 3076
  13.0 5.3 %collective-permute-start.6 = (f32[1,16,256]{2,1,0:T(8,128)S(1)}, f32[1,16,256]{2,1,0:T(8,128)S(1)}, u32[]{:S(2)}, u32[]{:S(2)}) collective-permute-start(f32[1,16,256]{2,1,0:T(8,128)S(1)} %bitcast.11), channel_id=1, source_target_pairs={{0,2},{2,0},{4,6},{6,4},{8,10},{10,8},{12,14},{14,12},{1,3},{3,1},... | collective-permute-start | bytes 49160 | tf_op jit(solution)/shard_map/ppermute | solution.py:28
  15.4 8.4 %collective-permute-start.3 = (bf16[288,256]{1,0:T(8,128)(2,1)S(1)}, bf16[288,256]{1,0:T(8,128)(2,1)S(1)}, u32[]{:S(2)}, u32[]{:S(2)}) collective-permute-start(bf16[288,256]{1,0:T(8,128)(2,1)S(1)} %collective-permute-done.2.half_ref), channel_id=1, source_target_pairs={{0,1},{1,0},{2,3},{3,2},{4,5},{5,4},{6,7},{7,6},{8,9},{9,8},{10,11... | collective-permute-start | bytes 442376 | tf_op jit(solution)/shard_map/ppermute | solution.py:33
  15.7 8.2 %collective-permute-start.4 = (bf16[80,576]{1,0:T(8,128)(2,1)S(1)}, bf16[80,576]{1,0:T(8,128)(2,1)S(1)}, u32[]{:S(2)}, u32[]{:S(2)}) collective-permute-start(bf16[80,576]{1,0:T(8,128)(2,1)S(1)} %get-tuple-element.6.packed_ref), channel_id=1, source_target_pairs={{0,8},{2,10},{4,12},{6,14},{8,0},{10,2},{12,4},{14,6},{1,9},{3,11}... | collective-permute-start | bytes 276488 | tf_op jit(solution)/shard_map/ppermute | solution.py:28
  18.3 7.2 %collective-permute-start.7 = (f32[2,16,256]{2,1,0:T(8,128)S(1)}, f32[2,16,256]{2,1,0:T(8,128)S(1)}, u32[]{:S(2)}, u32[]{:S(2)}) collective-permute-start(f32[2,16,256]{2,1,0:T(8,128)S(1)} %pad_maximum_fusion.1), channel_id=1, source_target_pairs={{0,4},{2,6},{4,0},{6,2},{8,12},{10,14},{12,8},{14,10},{1,5},{3,7},... | collective-permute-start | bytes 98312 | tf_op jit(solution)/shard_map/ppermute | solution.py:28
  24.6 10.9 %collective-permute-start.5 = (bf16[64,640]{1,0:T(8,128)(2,1)S(1)}, bf16[64,640]{1,0:T(8,128)(2,1)S(1)}, u32[]{:S(2)}, u32[]{:S(2)}) collective-permute-start(bf16[64,640]{1,0:T(8,128)(2,1)S(1)} %shard_map.79), channel_id=1, source_target_pairs={{0,8},{2,10},{4,12},{6,14},{8,0},{10,2},{12,4},{14,6},{1,9},{3,11}... | collective-permute-start | bytes 245768 | tf_op jit(solution)/shard_map/ppermute | solution.py:28
  25.5 8.5 %collective-permute-start.8 = (f32[4,16,256]{2,1,0:T(8,128)S(1)}, f32[4,16,256]{2,1,0:T(8,128)S(1)}, u32[]{:S(2)}, u32[]{:S(2)}) collective-permute-start(f32[4,16,256]{2,1,0:T(8,128)S(1)} %pad_maximum_fusion.refs_0_), channel_id=1, source_target_pairs={{0,8},{2,10},{4,12},{6,14},{8,0},{10,2},{12,4},{14,6},{1,9},{3,11}... | collective-permute-start | bytes 196616 | tf_op jit(solution)/shard_map/ppermute | solution.py:28

commit v2 on v1

--- a/solution.py
+++ b/solution.py
@@ -11,6 +11,7 @@
 LATENT = 512
 LANES = 128
 SPAN = 4
+TAIL_ROWS = 16
 
 score_scale = 192.0 ** (-0.5)
 floor_value = -1e30
@@ -53,13 +54,32 @@
     )
 
 
-def prepare_kernel(query_ref, index_query_ref, weight_ref, keys_ref, list_ref, packed_ref, share_ref):
+def fetch(refs, held_refs, sems):
+    copies = [pltpu.make_async_copy(ref, held, sems.at[j]) for j, (ref, held) in enumerate(zip(refs, held_refs))]
+    for copy in copies:
+        copy.start()
+    return copies
+
+
+def prepare_kernel(
+    list_ref, query_ref, latent_ref, index_query_ref, weight_ref, keys_ref,
+    packed_ref, half_ref, share_ref,
+    list_held, query_held, index_query_held, weight_held, keys_held, sems, wide_ref,
+):
     keys_here, width = keys_ref.shape
     rows, head_count = weight_ref.shape
     shards = share_ref.shape[0] - rows
     top_count = list_ref.shape[1]
-    row_width = query_ref.shape[1]
-    places = list_ref[...]
+    half_rows = half_ref.shape[0]
+    odd = lax.axis_index("pb") % 2
+    source = latent_ref.at[pl.ds(pl.multiple_of(odd * half_rows, 16), half_rows), :]
+    list_copy, query_copy, index_copy, weight_copy, keys_copy, half_copy = fetch(
+        (list_ref, query_ref, index_query_ref, weight_ref, keys_ref, source),
+        (list_held, query_held, index_query_held, weight_held, keys_held, half_ref),
+        sems,
+    )
+    list_copy.wait()
+    places = list_held[...]
     low = places % LANES
     high = places // LANES
     low_hot = (lax.broadcasted_iota(jnp.int32, (LANES, top_count), 0) == low).astype(jnp.bfloat16)
@@ -70,36 +90,58 @@
         high_hot = (owner + part == high).astype(jnp.bfloat16)
         parts.append(lax.dot_general(high_hot, low_hot, NT, preferred_element_type=jnp.float32))
     mask = jnp.concatenate(parts, axis=1)
-    pad_rows = packed_ref.shape[0] - HEADS - shards
-    wide = jnp.concatenate([mask, jnp.zeros((shards, row_width - keys_here), jnp.float32)], axis=1)
-    if pad_rows:
-        wide = jnp.concatenate([wide, jnp.zeros((pad_rows, row_width), jnp.float32)], axis=0)
-    packed_ref[HEADS:, :] = wide.astype(jnp.bfloat16)
-    packed_ref[:HEADS, :] = query_ref[...]
+    query_copy.wait()
+    pair_count, pair_width = wide_ref.shape
+    row_width = pair_width // 2
+    for p in range(pair_count):
+        wide_ref[p : p + 1, :] = query_held[:, p * pair_width : (p + 1) * pair_width].astype(jnp.float32)
+    wide = wide_ref[...]
+    packed_ref[:pair_count, :] = wide[:, :LATENT].astype(jnp.bfloat16)
+    packed_ref[pair_count:HEADS, :] = wide[:, row_width : row_width + LATENT].astype(jnp.bfloat16)
+    rope = jnp.concatenate([wide[:, LATENT:row_width], wide[:, row_width + LATENT :]], axis=0)
+    rope = jnp.concatenate([rope[g : g + TAIL_ROWS] for g in range(0, HEADS, TAIL_ROWS)], axis=1)
+    tail_rows = packed_ref.shape[0] - HEADS
+    packed_ref[HEADS:, : rope.shape[1]] = padded(rope, tail_rows).astype(jnp.bfloat16)
+    packed_ref[HEADS:, LATENT - keys_here :] = padded(mask, tail_rows).astype(jnp.bfloat16)
+    index_copy.wait()
+    weight_copy.wait()
+    keys_copy.wait()
     stacked = jnp.concatenate(
-        [index_query_ref[:, h * width : (h + 1) * width].astype(jnp.float32) for h in range(head_count)], axis=0
+        [index_query_held[:, h * width : (h + 1) * width].astype(jnp.float32) for h in range(head_count)], axis=0
     ).astype(jnp.bfloat16)
-    products = lax.dot_general(stacked, keys_ref[...], NT, preferred_element_type=jnp.float32)
+    products = lax.dot_general(stacked, keys_held[...], NT, preferred_element_type=jnp.float32)
     total = jnp.zeros((rows, keys_here), jnp.float32)
     for h in range(head_count):
-        total += weight_ref[:, h : h + 1] * jnp.maximum(products[h * rows : (h + 1) * rows], 0.0)
+        total += weight_held[:, h : h + 1] * jnp.maximum(products[h * rows : (h + 1) * rows], 0.0)
     share_ref[:rows, :] = total * float(head_count * width) ** (-0.5)
     share_ref[rows:, :] = mask
+    half_copy.wait()
+
+
+def padded(x, rows):
+    if x.shape[0] == rows:
+        return x
+    return jnp.concatenate([x, jnp.zeros((rows - x.shape[0], x.shape[1]), x.dtype)], axis=0)
 
 
 def attend(packed_ref, row_refs, far_ref, mask_ref):
     me = lax.axis_index("ctx")
     odd = lax.axis_index("pb") % 2
     keys_here = row_refs[0].shape[1]
+    rope_width = far_ref.shape[0] - LATENT
     owners = [me, me ^ (1 + odd), me ^ (2 - odd), me ^ 3]
-    mask_ref[...] = packed_ref[HEADS:, :keys_here].astype(jnp.float32)
-    queries = packed_ref[:HEADS, :]
+    mask_ref[...] = packed_ref[HEADS:, LATENT - keys_here :].astype(jnp.float32)
+    latent = packed_ref[:HEADS, :]
+    tail = packed_ref[HEADS : HEADS + TAIL_ROWS, :]
+    groups = HEADS // TAIL_ROWS
+    rope = jnp.concatenate([tail[:, g * rope_width : (g + 1) * rope_width] for g in range(groups)], axis=0)
     refs = list(row_refs) + [far_ref]
     pieces = []
     for owner, ref in zip(owners, refs):
-        piece = lax.dot_general(queries, ref[...], NN, preferred_element_type=jnp.float32) * score_scale
+        piece = lax.dot_general(latent, ref[:LATENT, :], NN, preferred_element_type=jnp.float32)
+        piece += lax.dot_general(rope, ref[LATENT:, :], NN, preferred_element_type=jnp.float32)
         keep = mask_ref[pl.ds(owner, 1), :] > 0.5
-        pieces.append(jnp.where(keep, piece, floor_value))
+        pieces.append(jnp.where(keep, piece * score_scale, floor_value))
     scores = jnp.concatenate(pieces, axis=1)
     highest = jnp.max(scores, axis=1, keepdims=True)
     expo = jnp.where(scores > 0.5 * floor_value, jnp.exp(scores - highest), 0.0)
@@ -113,6 +155,32 @@
     some = total > 0.0
     safe = jnp.where(some, total, 1.0)
     return mixed / safe, jnp.where(some, highest + jnp.log(safe), floor_value)
+
+
+def hold(x, flops):
+    return call(
+        lambda x_ref, out_ref: None,
+        jax.ShapeDtypeStruct(x.shape, x.dtype),
+        in_specs=[pl.BlockSpec(memory_space=pl.ANY)],
+        out_specs=pl.BlockSpec(memory_space=pl.ANY),
+        input_output_aliases={0: 0},
+        cost_estimate=pl.CostEstimate(flops=flops, bytes_accessed=0, transcendentals=0),
+    )(x)
+
+
+def join_kernel(left_ref, right_ref, after_ref, out_ref):
+    count = left_ref.shape[0]
+    out_ref[:count] = left_ref[...]
+    out_ref[count:] = right_ref[...]
+
+
+def join(left, right, after):
+    in_vmem = pl.BlockSpec(memory_space=pltpu.VMEM)
+    return call(
+        join_kernel,
+        jax.ShapeDtypeStruct((left.shape[0] + right.shape[0], *left.shape[1:]), left.dtype),
+        in_specs=[in_vmem, in_vmem, pl.BlockSpec(memory_space=pl.ANY)],
+    )(left, right, after)
 
 
 def fill_far(half_ref, other_ref, far_ref):
@@ -157,7 +225,10 @@
     weights = [jnp.exp(lse - peak) for lse in lses]
     total = functools.reduce(jnp.add, weights)
     mixed = functools.reduce(jnp.add, [w * m for w, m in zip(weights, mixes)])
-    out_ref[...] = (mixed / total).astype(jnp.bfloat16)
+    done = (mixed / total).astype(jnp.bfloat16)
+    for h in range(HEADS):
+        row = h // 2 + (h % 2) * (HEADS // 2)
+        out_ref[:, h * LATENT : (h + 1) * LATENT] = done[row : row + 1, :]
 
 
 def share_kernel(offsets, first_place, *refs):
@@ -202,15 +273,23 @@
 
     latent = latent_cache.T
     near = swap_apart(latent, 1, 2)
+
+    packed_rows = HEADS + round_up(max(shards, TAIL_ROWS), 16)
     half_rows = row_width // 2
-    half = lax.dynamic_slice_in_dim(latent, (lax.axis_index("pb") % 2) * half_rows, half_rows, 0)
+    inputs = (selected[0], att_query[0], latent, index_query[0], index_weight[0], index_keys)
+    inputs = [pltpu.with_memory_space_constraint(x, pltpu.HBM) for x in inputs]
+    held = [pltpu.VMEM(x.shape, x.dtype) for x in (selected[0], att_query[0], index_query[0], index_weight[0], index_keys)]
+    packed, half, share_own = call(
+        prepare_kernel,
+        (
+            shape((packed_rows, LATENT), bf16),
+            shape((half_rows, keys_here), bf16),
+            shape((rows + shards, keys_here), f32),
+        ),
+        (*held, pltpu.SemaphoreType.DMA((6,)), pltpu.VMEM((HEADS // 2, 2 * row_width), f32)),
+        in_specs=[pl.BlockSpec(memory_space=pltpu.HBM)] * len(inputs),
+    )(*inputs)
     far_half = swap(half, 3)
-
-    packed_rows = HEADS + round_up(shards, 16)
-    packed, share_own = call(
-        prepare_kernel,
-        (shape((packed_rows, row_width), bf16), shape((rows + shards, keys_here), f32)),
-    )(att_query.reshape(HEADS, row_width), index_query[0], index_weight[0], index_keys, selected[0])
 
     near_other = swap_cores(near)
     far_other = swap_cores(far_half)
@@ -219,28 +298,30 @@
     scratch = (pltpu.VMEM((row_width, keys_here), bf16), pltpu.VMEM((packed_rows - HEADS, keys_here), f32))
     parts = []
     for k in range(1, shards // SPAN):
-        asked = swap(packed, SPAN * k)
-        part = call(send_kernel, shape((HEADS, LATENT + LANES), bf16), scratch)(asked, *span_rows)
-        parts.append(swap(part, SPAN * k))
+        asked = hold(swap(packed, SPAN * k), 3000000000)
+        sent = call(send_kernel, shape((HEADS, LATENT + LANES), bf16), scratch)(asked, *span_rows)
+        parts.append(hold(swap(sent, SPAN * k), 10000000000))
     kept, kept_lse = call(
         keep_kernel, (shape((HEADS, LATENT), f32), shape((HEADS, LANES), f32)), scratch
     )(packed, *span_rows)
-    attended = call(combine_kernel, shape((HEADS, LATENT), bf16))(kept, kept_lse, *parts)
+    attended = call(combine_kernel, shape((1, HEADS * LATENT), bf16))(kept, kept_lse, *parts)
 
     held, offsets = share_own[None], [0]
-    bits = [1 << b for b in range(shards.bit_length() - 1)]
+    bits = [1 << b for b in range(2, shards.bit_length() - 1)] + [1, 2]
     arrived = held
-    for bit in bits:
-        if bit != bits[0]:
-            held = jnp.concatenate([held, arrived], axis=0)
+    for step, bit in enumerate(bits):
+        if step:
+            held = join(held, arrived, share_own if step < 2 else sent)
         arrived = swap(held, bit)
+        if not step:
+            arrived = hold(arrived, 20000000000)
         offsets = offsets + [o ^ bit for o in offsets]
     log_share = call(
         functools.partial(share_kernel, offsets, keys_here * shards - rows * blocks),
         shape((1, rows), f32),
         (pltpu.VMEM((shards, rows, keys_here), f32), pltpu.VMEM((shards, shards, keys_here), f32)),
     )(held, arrived)
-    return attended.reshape(1, 1, HEADS * LATENT), log_share
+    return attended[None], log_share
 
 
 def solution(mesh):

time: 36.7 us -> 25.3 us (0.69)
  waiting for transfers between devices: 15.4 us -> 7.06 us
  local copies, waits for them, and re-layouts: 2.5 us -> 0.01 us
  starting transfers between devices: 14.5 us -> 12.6 us
  Pallas kernels: 2.93 us -> 4.77 us
  other arithmetic: 0.43 us -> 0 us
    ppermute x1, waiting for transfers between devices: 5.1 us -> 0.01 us  [swap_apart(): return lax.ppermute(x, ('ctx', 'pb'), moves)]
    ppermute x6, waiting for transfers between devices: 10.3 us -> 7.05 us  [swap(): return lax.ppermute(x, 'ctx', [(i, i ^ offset) for i in range(size)])]
    pallas_call x2 -> x7, Pallas kernels: 0.55 us -> 2.32 us  [the longest x1 1.45 us: body(): call(prepare_kernel, (shape((packed_rows, LATENT), bf16), shape((half_row...]
    ppermute x6, starting transfers between devices: 11.3 us -> 9.64 us  [swap(): return lax.ppermute(x, 'ctx', [(i, i ^ offset) for i in range(size)])]
    dynamic_slice x1 -> x0, local copies, waits for them, and re-layouts: 0.99 us -> none  [body(): lax.dynamic_slice_in_dim(latent, lax.axis_index('pb') % 2 * half_rows, ha...]
    reshape x2 -> x0, local copies, waits for them, and re-layouts: 0.81 us -> none  [the longest x1 0.69 us: body(): return (attended.reshape(1, 1, HEADS * LATENT), log_share)]
    unnamed x12 -> x2, local copies, waits for them, and re-layouts: 0.71 us -> 0.01 us
    unnamed x1 -> x0, other arithmetic: 0.42 us -> none
  transfers between devices with their start and end apart: 9 -> 9, of which waited for: 3 -> 4; matrix products, arithmetic and copies ran while one was open for 4% -> 0% of each run, Pallas kernels for 8% -> 16%
where the time goes in v2:
time: 25.3 us; the launch traced here: 25.1 us
  starting transfers between devices  12.6 us (50%)
  waiting for transfers between devices  7.06 us (28%)
  Pallas kernels  4.77 us (19%)
  between operations  0.66 us (3%)
    ppermute x6, starting transfers between devices, swap(): return lax.ppermute(x, 'ctx', [(i, i ^ offset) for i in range(size)])  9.64 us
    ppermute x6, waiting for transfers between devices, swap(): return lax.ppermute(x, 'ctx', [(i, i ^ offset) for i in range(size)])  7.05 us
    ppermute x1, starting transfers between devices, swap_apart(): return lax.ppermute(x, ('ctx', 'pb'), moves)  3 us
    pallas_call x1, Pallas kernels, body(): call(prepare_kernel, (shape((packed_rows, LATENT), bf16), shape((half_row...  1.45 us
    pallas_call x1, Pallas kernels, body(): call(combine_kernel, shape((1, HEADS * LATENT), bf16))  0.86 us
    pallas_call x1, Pallas kernels, body(): call(send_kernel, shape((HEADS, LATENT + LANES), bf16), scratch)  0.84 us
    pallas_call x1, Pallas kernels, body(): call(keep_kernel, (shape((HEADS, LATENT), f32), shape((HEADS, LANES), f32...  0.83 us
    pallas_call x1, Pallas kernels, body(): call(functools.partial(share_kernel, offsets, keys_here * shards - rows *...  0.78 us
  transfers between devices with their start and end apart: 9, of which 4 were waited for; matrix products, arithmetic and copies ran while one was open for 0% of the time, Pallas kernels for 16%

profile of v2, /device:TPU:0, one launch (start us, length us, event | category | flops | bytes accessed | tf_op | source)
XLA Modules:
  0.0 25.1 jit_solution(9802202663901592727)
XLA Ops:
  0.6 3.0 %collective-permute-start = (bf16[576,256]{1,0:T(8,128)(2,1)}, bf16[576,256]{1,0:T(8,128)(2,1)S(1)}, u32[]{:S(2)}, u32[]{:S(2)}) collective-permute-start(bf16[576,256]{1,0:T(8,128)(2,1)} %bitcast.7), channel_id=1, source_target_pairs={{0,2},{1,5},{2,0},{3,7},{4,6},{5,1},{6,4},{7,3},{8,10},{9,13},{10,... | collective-permute-start | bytes 884744 | tf_op jit(solution)/shard_map/ppermute | solution.py:44
  3.6 1.4 %shard_map.77 = (bf16[80,512]{1,0:T(8,128)(2,1)S(1)}, bf16[288,256]{1,0:T(8,128)(2,1)S(1)}, f32[16,256]{1,0:T(8,128)S(1)}) custom-call(s32[1,1024]{1,0:T(1,128)} %bitcast.16, bf16[1,36864]{1,0:T(2,128)(2,1)} %bitcast.13, bf16[576,256]{1,0:T(8,128)(2,1)} %bitcast.8, bf16[8,4096]{1,0:T(8,128)(2,1)} %bitcast.15, f32[8,32]{1,0:T(8,128)} %bitcast.17, ...), custom_call_target="tpu_custom_call" | custom-call | tf_op jit(solution)/shard_map/pallas_call | solution.py:282
  5.1 2.7 %collective-permute-start.6 = (f32[1,16,256]{2,1,0:T(8,128)S(1)}, f32[1,16,256]{2,1,0:T(8,128)S(1)}, u32[]{:S(2)}, u32[]{:S(2)}) collective-permute-start(f32[1,16,256]{2,1,0:T(8,128)S(1)} %bitcast.11), channel_id=1, source_target_pairs={{0,8},{2,10},{4,12},{6,14},{8,0},{10,2},{12,4},{14,6},{1,9},{3,11}... | collective-permute-start | bytes 49160 | tf_op jit(solution)/shard_map/ppermute | solution.py:29
  7.7 1.5 %collective-permute-start.2 = (bf16[288,256]{1,0:T(8,128)(2,1)S(1)}, bf16[288,256]{1,0:T(8,128)(2,1)S(1)}, u32[]{:S(2)}, u32[]{:S(2)}) collective-permute-start(bf16[288,256]{1,0:T(8,128)(2,1)S(1)} %get-tuple-element.8), channel_id=1, source_target_pairs={{0,6},{2,4},{4,2},{6,0},{8,14},{10,12},{12,10},{14,8},{1,7},{3,5},... | collective-permute-start | bytes 442376 | tf_op jit(solution)/shard_map/ppermute | solution.py:29
  9.3 0.3 %collective-permute-start.4 = (bf16[80,512]{1,0:T(8,128)(2,1)S(1)}, bf16[80,512]{1,0:T(8,128)(2,1)S(1)}, u32[]{:S(2)}, u32[]{:S(2)}) collective-permute-start(bf16[80,512]{1,0:T(8,128)(2,1)S(1)} %get-tuple-element.7.packed_ref), channel_id=1, source_target_pairs={{0,8},{2,10},{4,12},{6,14},{8,0},{10,2},{12,4},{14,6},{1,9},{3,11}... | collective-permute-start | bytes 245768 | tf_op jit(solution)/shard_map/ppermute | solution.py:29
  9.6 0.0 collective-permute-done.first_ref
  9.6 0.0 collective-permute-start.1
  9.6 0.2 collective-permute-done.6.x_ref
  9.8 0.0 copy-start
  9.8 1.4 %collective-permute-start.7 = (f32[2,16,256]{2,1,0:T(8,128)S(1)}, f32[2,16,256]{2,1,0:T(8,128)S(1)}, u32[]{:S(2)}, u32[]{:S(2)}) collective-permute-start(f32[2,16,256]{2,1,0:T(8,128)S(1)} %shard_map.84.left_ref), channel_id=1, source_target_pairs={{0,2},{2,0},{4,6},{6,4},{8,10},{10,8},{12,14},{14,12},{1,3},{3,1},... | collective-permute-start | bytes 98312 | tf_op jit(solution)/shard_map/ppermute | solution.py:29
  11.2 3.5 %collective-permute-done.2.half_ref = bf16[288,256]{1,0:T(8,128)(2,1)S(1)} collective-permute-done((bf16[288,256]{1,0:T(8,128)(2,1)S(1)}, bf16[288,256]{1,0:T(8,128)(2,1)S(1)}, u32[]{:S(2)}, u32[]{:S(2)}) %collective-permute-start.2) | collective-permute-done | bytes 147488 | tf_op jit(solution)/shard_map/ppermute | solution.py:29
  14.7 0.0 collective-permute-start.3
  14.7 1.5 %collective-permute-done.4.x_ref = bf16[80,512]{1,0:T(8,128)(2,1)S(1)} collective-permute-done((bf16[80,512]{1,0:T(8,128)(2,1)S(1)}, bf16[80,512]{1,0:T(8,128)(2,1)S(1)}, u32[]{:S(2)}, u32[]{:S(2)}) %collective-permute-start.4) | collective-permute-done | bytes 81952 | tf_op jit(solution)/shard_map/ppermute | solution.py:29
  16.2 0.0 collective-permute-done.3.other_ref
  16.2 0.0 collective-permute-done.1.second_ref
  16.2 0.0 copy-done
  16.2 0.8 %shard_map.80.after_ref = bf16[64,640]{1,0:T(8,128)(2,1)S(1)} custom-call(bf16[80,512]{1,0:T(8,128)(2,1)S(1)} %shard_map.79.packed_ref, bf16[576,256]{1,0:T(8,128)(2,1)S(1)} %bitcast.9, bf16[576,256]{1,0:T(8,128)(2,1)S(1)} %collective-permute-done.first_ref, bf16[576,256]{1,0:T(8,128)(2,1)S(1)} %collective-permute-done.1.second_ref, ...), custom_call_target="tpu_custom_call" | custom-call | tf_op jit(solution)/shard_map/pallas_call | solution.py:302
  17.0 1.6 %collective-permute-start.5 = (bf16[64,640]{1,0:T(8,128)(2,1)S(1)}, bf16[64,640]{1,0:T(8,128)(2,1)S(1)}, u32[]{:S(2)}, u32[]{:S(2)}) collective-permute-start(bf16[64,640]{1,0:T(8,128)(2,1)S(1)} %shard_map.80.after_ref), channel_id=1, source_target_pairs={{0,8},{2,10},{4,12},{6,14},{8,0},{10,2},{12,4},{14,6},{1,9},{3,11}... | collective-permute-start | bytes 245768 | tf_op jit(solution)/shard_map/ppermute | solution.py:29
  18.7 0.0 collective-permute-done.7.right_ref
  18.7 2.0 %collective-permute-start.8 = (f32[4,16,256]{2,1,0:T(8,128)S(1)}, f32[4,16,256]{2,1,0:T(8,128)S(1)}, u32[]{:S(2)}, u32[]{:S(2)}) collective-permute-start(f32[4,16,256]{2,1,0:T(8,128)S(1)} %shard_map.85.refs_0_), channel_id=1, source_target_pairs={{0,4},{2,6},{4,0},{6,2},{8,12},{10,14},{12,8},{14,10},{1,5},{3,7},... | collective-permute-start | bytes 196616 | tf_op jit(solution)/shard_map/ppermute | solution.py:29
  20.7 0.8 %shard_map.78 = (f32[64,512]{1,0:T(8,128)S(1)}, f32[64,128]{1,0:T(8,128)S(1)}) custom-call(bf16[80,512]{1,0:T(8,128)(2,1)S(1)} %get-tuple-element.7.packed_ref, bf16[576,256]{1,0:T(8,128)(2,1)S(1)} %bitcast.10, bf16[576,256]{1,0:T(8,128)(2,1)S(1)} %collective-permute-done.first_ref, bf16[576,256]{1,0:T(8,128)(2,1)S(1)} %collective-permute-done.1.second_ref, ...), custom_call_target="tpu_custom_call" | custom-call | tf_op jit(solution)/shard_map/pallas_call | solution.py:304
  21.6 1.9 %collective-permute-done.8.refs_1_ = f32[4,16,256]{2,1,0:T(8,128)S(1)} collective-permute-done((f32[4,16,256]{2,1,0:T(8,128)S(1)}, f32[4,16,256]{2,1,0:T(8,128)S(1)}, u32[]{:S(2)}, u32[]{:S(2)}) %collective-permute-start.8) | collective-permute-done | bytes 65568 | tf_op jit(solution)/shard_map/ppermute | solution.py:29
  23.5 0.8 %shard_map.86 = f32[1,8]{1,0:T(1,128)} custom-call(f32[4,16,256]{2,1,0:T(8,128)S(1)} %shard_map.85.refs_0_, f32[4,16,256]{2,1,0:T(8,128)S(1)} %collective-permute-done.8.refs_1_), custom_call_target="tpu_custom_call" | custom-call | tf_op jit(solution)/shard_map/pallas_call | solution.py:319
  24.3 0.0 collective-permute-done.5.x_ref
  24.3 0.9 %shard_map.82 = bf16[1,32768]{1,0:T(2,128)(2,1)} custom-call(f32[64,512]{1,0:T(8,128)S(1)} %get-tuple-element.9.own_ref, f32[64,128]{1,0:T(8,128)S(1)} %get-tuple-element.10.lse_ref, bf16[64,640]{1,0:T(8,128)(2,1)S(1)} %shard_map.81.refs_0_), custom_call_target="tpu_custom_call" | custom-call | tf_op jit(solution)/shard_map/pallas_call | solution.py:307
  (5 shorter events, 0.0 us)
Async XLA Ops:
  0.6 9.0 %collective-permute-start = (bf16[576,256]{1,0:T(8,128)(2,1)}, bf16[576,256]{1,0:T(8,128)(2,1)S(1)}, u32[]{:S(2)}, u32[]{:S(2)}) collective-permute-start(bf16[576,256]{1,0:T(8,128)(2,1)} %bitcast.7), channel_id=1, source_target_pairs={{0,2},{1,5},{2,0},{3,7},{4,6},{5,1},{6,4},{7,3},{8,10},{9,13},{10,... | collective-permute-start | bytes 884744 | tf_op jit(solution)/shard_map/ppermute | solution.py:44
  5.1 4.7 %collective-permute-start.6 = (f32[1,16,256]{2,1,0:T(8,128)S(1)}, f32[1,16,256]{2,1,0:T(8,128)S(1)}, u32[]{:S(2)}, u32[]{:S(2)}) collective-permute-start(f32[1,16,256]{2,1,0:T(8,128)S(1)} %bitcast.11), channel_id=1, source_target_pairs={{0,8},{2,10},{4,12},{6,14},{8,0},{10,2},{12,4},{14,6},{1,9},{3,11}... | collective-permute-start | bytes 49160 | tf_op jit(solution)/shard_map/ppermute | solution.py:29
  7.7 7.0 %collective-permute-start.2 = (bf16[288,256]{1,0:T(8,128)(2,1)S(1)}, bf16[288,256]{1,0:T(8,128)(2,1)S(1)}, u32[]{:S(2)}, u32[]{:S(2)}) collective-permute-start(bf16[288,256]{1,0:T(8,128)(2,1)S(1)} %get-tuple-element.8), channel_id=1, source_target_pairs={{0,6},{2,4},{4,2},{6,0},{8,14},{10,12},{12,10},{14,8},{1,7},{3,5},... | collective-permute-start | bytes 442376 | tf_op jit(solution)/shard_map/ppermute | solution.py:29
  9.3 6.9 %collective-permute-start.4 = (bf16[80,512]{1,0:T(8,128)(2,1)S(1)}, bf16[80,512]{1,0:T(8,128)(2,1)S(1)}, u32[]{:S(2)}, u32[]{:S(2)}) collective-permute-start(bf16[80,512]{1,0:T(8,128)(2,1)S(1)} %get-tuple-element.7.packed_ref), channel_id=1, source_target_pairs={{0,8},{2,10},{4,12},{6,14},{8,0},{10,2},{12,4},{14,6},{1,9},{3,11}... | collective-permute-start | bytes 245768 | tf_op jit(solution)/shard_map/ppermute | solution.py:29
  9.6 6.6 %collective-permute-start.1 = (bf16[576,256]{1,0:T(8,128)(2,1)S(1)}, bf16[576,256]{1,0:T(8,128)(2,1)S(1)}, u32[]{:S(2)}, u32[]{:S(2)}) collective-permute-start(bf16[576,256]{1,0:T(8,128)(2,1)S(1)} %collective-permute-done.first_ref), channel_id=1, source_target_pairs={{0,1},{1,0},{2,3},{3,2},{4,5},{5,4},{6,7},{7,6},{8,9},{9,8},{10,11... | collective-permute-start | bytes 884744 | tf_op jit(solution)/shard_map/ppermute | solution.py:34
  9.8 6.4 %copy-start = (bf16[256,576]{0,1:T(8,128)(2,1)S(1)}, bf16[256,576]{0,1:T(8,128)(2,1)}, u32[]{:S(2)}) copy-start(bf16[256,576]{0,1:T(8,128)(2,1)} %param.7) | copy-start | bytes 884740
  9.8 8.9 %collective-permute-start.7 = (f32[2,16,256]{2,1,0:T(8,128)S(1)}, f32[2,16,256]{2,1,0:T(8,128)S(1)}, u32[]{:S(2)}, u32[]{:S(2)}) collective-permute-start(f32[2,16,256]{2,1,0:T(8,128)S(1)} %shard_map.84.left_ref), channel_id=1, source_target_pairs={{0,2},{2,0},{4,6},{6,4},{8,10},{10,8},{12,14},{14,12},{1,3},{3,1},... | collective-permute-start | bytes 98312 | tf_op jit(solution)/shard_map/ppermute | solution.py:29
  14.7 1.5 %collective-permute-start.3 = (bf16[288,256]{1,0:T(8,128)(2,1)S(1)}, bf16[288,256]{1,0:T(8,128)(2,1)S(1)}, u32[]{:S(2)}, u32[]{:S(2)}) collective-permute-start(bf16[288,256]{1,0:T(8,128)(2,1)S(1)} %collective-permute-done.2.half_ref), channel_id=1, source_target_pairs={{0,1},{1,0},{2,3},{3,2},{4,5},{5,4},{6,7},{7,6},{8,9},{9,8},{10,11... | collective-permute-start | bytes 442376 | tf_op jit(solution)/shard_map/ppermute | solution.py:34
  17.0 7.2 %collective-permute-start.5 = (bf16[64,640]{1,0:T(8,128)(2,1)S(1)}, bf16[64,640]{1,0:T(8,128)(2,1)S(1)}, u32[]{:S(2)}, u32[]{:S(2)}) collective-permute-start(bf16[64,640]{1,0:T(8,128)(2,1)S(1)} %shard_map.80.after_ref), channel_id=1, source_target_pairs={{0,8},{2,10},{4,12},{6,14},{8,0},{10,2},{12,4},{14,6},{1,9},{3,11}... | collective-permute-start | bytes 245768 | tf_op jit(solution)/shard_map/ppermute | solution.py:29
  18.7 4.8 %collective-permute-start.8 = (f32[4,16,256]{2,1,0:T(8,128)S(1)}, f32[4,16,256]{2,1,0:T(8,128)S(1)}, u32[]{:S(2)}, u32[]{:S(2)}) collective-permute-start(f32[4,16,256]{2,1,0:T(8,128)S(1)} %shard_map.85.refs_0_), channel_id=1, source_target_pairs={{0,4},{2,6},{4,0},{6,2},{8,12},{10,14},{12,8},{14,10},{1,5},{3,7},... | collective-permute-start | bytes 196616 | tf_op jit(solution)/shard_map/ppermute | solution.py:29

commit v3 on v2

--- a/solution.py
+++ b/solution.py
@@ -62,20 +62,17 @@
 
 
 def prepare_kernel(
-    list_ref, query_ref, latent_ref, index_query_ref, weight_ref, keys_ref,
-    packed_ref, half_ref, share_ref,
+    list_ref, query_ref, index_query_ref, weight_ref, keys_ref,
+    packed_ref, share_ref,
     list_held, query_held, index_query_held, weight_held, keys_held, sems, wide_ref,
 ):
     keys_here, width = keys_ref.shape
     rows, head_count = weight_ref.shape
     shards = share_ref.shape[0] - rows
     top_count = list_ref.shape[1]
-    half_rows = half_ref.shape[0]
-    odd = lax.axis_index("pb") % 2
-    source = latent_ref.at[pl.ds(pl.multiple_of(odd * half_rows, 16), half_rows), :]
-    list_copy, query_copy, index_copy, weight_copy, keys_copy, half_copy = fetch(
-        (list_ref, query_ref, index_query_ref, weight_ref, keys_ref, source),
-        (list_held, query_held, index_query_held, weight_held, keys_held, half_ref),
+    list_copy, query_copy, index_copy, weight_copy, keys_copy = fetch(
+        (list_ref, query_ref, index_query_ref, weight_ref, keys_ref),
+        (list_held, query_held, index_query_held, weight_held, keys_held),
         sems,
     )
     list_copy.wait()
@@ -91,11 +88,11 @@
         parts.append(lax.dot_general(high_hot, low_hot, NT, preferred_element_type=jnp.float32))
     mask = jnp.concatenate(parts, axis=1)
     query_copy.wait()
-    pair_count, pair_width = wide_ref.shape
-    row_width = pair_width // 2
-    for p in range(pair_count):
-        wide_ref[p : p + 1, :] = query_held[:, p * pair_width : (p + 1) * pair_width].astype(jnp.float32)
-    wide = wide_ref[...]
+    wide_ref[...] = query_held[...].astype(jnp.float32).reshape(wide_ref.shape)
+    pair_count = HEADS // 2
+    row_width = query_ref.shape[1] // HEADS
+    tiles = wide_ref.shape[0] // pair_count
+    wide = jnp.concatenate([wide_ref[pl.ds(c, pair_count, stride=tiles), :] for c in range(tiles)], axis=1)
     packed_ref[:pair_count, :] = wide[:, :LATENT].astype(jnp.bfloat16)
     packed_ref[pair_count:HEADS, :] = wide[:, row_width : row_width + LATENT].astype(jnp.bfloat16)
     rope = jnp.concatenate([wide[:, LATENT:row_width], wide[:, row_width + LATENT :]], axis=0)
@@ -115,7 +112,6 @@
         total += weight_held[:, h : h + 1] * jnp.maximum(products[h * rows : (h + 1) * rows], 0.0)
     share_ref[:rows, :] = total * float(head_count * width) ** (-0.5)
     share_ref[rows:, :] = mask
-    half_copy.wait()
 
 
 def padded(x, rows):
@@ -124,18 +120,20 @@
     return jnp.concatenate([x, jnp.zeros((rows - x.shape[0], x.shape[1]), x.dtype)], axis=0)
 
 
-def attend(packed_ref, row_refs, far_ref, mask_ref):
+def span_owners():
     me = lax.axis_index("ctx")
     odd = lax.axis_index("pb") % 2
-    keys_here = row_refs[0].shape[1]
-    rope_width = far_ref.shape[0] - LATENT
-    owners = [me, me ^ (1 + odd), me ^ (2 - odd), me ^ 3]
+    return [me, me ^ (1 + odd), me ^ (2 - odd), me ^ 3]
+
+
+def attend(packed_ref, refs, owners, mask_ref):
+    keys_here = refs[0].shape[1]
+    rope_width = refs[0].shape[0] - LATENT
     mask_ref[...] = packed_ref[HEADS:, LATENT - keys_here :].astype(jnp.float32)
     latent = packed_ref[:HEADS, :]
     tail = packed_ref[HEADS : HEADS + TAIL_ROWS, :]
     groups = HEADS // TAIL_ROWS
     rope = jnp.concatenate([tail[:, g * rope_width : (g + 1) * rope_width] for g in range(groups)], axis=0)
-    refs = list(row_refs) + [far_ref]
     pieces = []
     for owner, ref in zip(owners, refs):
         piece = lax.dot_general(latent, ref[:LATENT, :], NN, preferred_element_type=jnp.float32)
@@ -152,20 +150,27 @@
         mixed += lax.dot_general(
             rounded[:, j * keys_here : (j + 1) * keys_here], ref[:LATENT, :], NT, preferred_element_type=jnp.float32
         )
+    return mixed, highest, total
+
+
+def finish(mixed, highest, total):
     some = total > 0.0
     safe = jnp.where(some, total, 1.0)
     return mixed / safe, jnp.where(some, highest + jnp.log(safe), floor_value)
 
 
-def hold(x, flops):
+def hold(x, flops=0, after=None):
+    if not flops and after is None:
+        return x
+    others = [] if after is None else [after]
     return call(
-        lambda x_ref, out_ref: None,
+        lambda *refs: None,
         jax.ShapeDtypeStruct(x.shape, x.dtype),
-        in_specs=[pl.BlockSpec(memory_space=pl.ANY)],
+        in_specs=[pl.BlockSpec(memory_space=pl.ANY)] * (1 + len(others)),
         out_specs=pl.BlockSpec(memory_space=pl.ANY),
         input_output_aliases={0: 0},
         cost_estimate=pl.CostEstimate(flops=flops, bytes_accessed=0, transcendentals=0),
-    )(x)
+    )(x, *others)
 
 
 def join_kernel(left_ref, right_ref, after_ref, out_ref):
@@ -183,41 +188,41 @@
     )(left, right, after)
 
 
-def fill_far(half_ref, other_ref, far_ref):
-    odd = lax.axis_index("pb") % 2
-    rows = half_ref.shape[0]
-    far_ref[pl.ds(pl.multiple_of(odd * rows, 16), rows), :] = half_ref[...]
-    far_ref[pl.ds(pl.multiple_of((1 - odd) * rows, 16), rows), :] = other_ref[...]
-
-
-def send_kernel(packed_ref, own_ref, first_ref, second_ref, half_ref, other_ref, out_ref, far_ref, mask_ref):
-    fill_far(half_ref, other_ref, far_ref)
-    mixed, lse = attend(packed_ref, (own_ref, first_ref, second_ref), far_ref, mask_ref)
-    high = lse.astype(jnp.bfloat16)
-    rest = lse - high.astype(jnp.float32)
-    middle = rest.astype(jnp.bfloat16)
-    last = (rest - middle.astype(jnp.float32)).astype(jnp.bfloat16)
+def begin_kernel(packed_ref, own_ref, first_ref, second_ref, mixed_ref, highest_ref, total_ref, mask_ref):
+    mixed, highest, total = attend(packed_ref, (own_ref, first_ref, second_ref), span_owners()[:3], mask_ref)
+    mixed_ref[...] = mixed
+    highest_ref[...] = jnp.broadcast_to(highest, highest_ref.shape)
+    total_ref[...] = jnp.broadcast_to(total, total_ref.shape)
+
+
+def send_kernel(packed_ref, far_ref, mixed_ref, highest_ref, total_ref, out_ref, mask_ref):
+    far_mixed, far_highest, far_total = attend(packed_ref, (far_ref,), span_owners()[3:], mask_ref)
+    highest = jnp.maximum(highest_ref[:, :1], far_highest)
+    scale, far_scale = jnp.exp(highest_ref[:, :1] - highest), jnp.exp(far_highest - highest)
+    total = total_ref[:, :1] * scale + far_total * far_scale
+    mixed, lse = finish(mixed_ref[...] * scale + far_mixed * far_scale, highest, total)
+    high, middle, low = split(lse)
     lane = lax.broadcasted_iota(jnp.int32, (HEADS, LANES), 1)
-    tail = jnp.where(
-        lane == 0,
-        high.astype(jnp.float32),
-        jnp.where(lane == 1, middle.astype(jnp.float32), last.astype(jnp.float32)),
-    )
+    tail = jnp.where(lane == 0, high, jnp.where(lane == 1, middle, low))
     out_ref[:, :LATENT] = mixed.astype(jnp.bfloat16)
     out_ref[:, LATENT:] = tail.astype(jnp.bfloat16)
 
 
-def keep_kernel(packed_ref, own_ref, first_ref, second_ref, half_ref, other_ref, out_ref, lse_ref, far_ref, mask_ref):
-    fill_far(half_ref, other_ref, far_ref)
-    mixed, lse = attend(packed_ref, (own_ref, first_ref, second_ref), far_ref, mask_ref)
+def keep_kernel(packed_ref, own_ref, first_ref, second_ref, far_ref, out_ref, lse_ref, mask_ref):
+    mixed, lse = finish(*attend(packed_ref, (own_ref, first_ref, second_ref, far_ref), span_owners(), mask_ref))
     out_ref[...] = mixed
     lse_ref[...] = jnp.broadcast_to(lse, lse_ref.shape)
 
 
-def combine_kernel(own_ref, lse_ref, *refs):
-    out_ref = refs[-1]
+def split(x):
+    high = x.astype(jnp.bfloat16).astype(jnp.float32)
+    middle = (x - high).astype(jnp.bfloat16).astype(jnp.float32)
+    return high, middle, x - high - middle
+
+
+def combine(own_ref, lse_ref, part_refs, out_ref, flat_ref):
     mixes, lses = [own_ref[...]], [lse_ref[:, :1]]
-    for ref in refs[:-1]:
+    for ref in part_refs:
         tail = ref[:, LATENT:].astype(jnp.float32)
         lses.append(tail[:, 0:1] + tail[:, 1:2] + tail[:, 2:3])
         mixes.append(ref[:, :LATENT].astype(jnp.float32))
@@ -225,14 +230,17 @@
     weights = [jnp.exp(lse - peak) for lse in lses]
     total = functools.reduce(jnp.add, weights)
     mixed = functools.reduce(jnp.add, [w * m for w, m in zip(weights, mixes)])
-    done = (mixed / total).astype(jnp.bfloat16)
-    for h in range(HEADS):
-        row = h // 2 + (h % 2) * (HEADS // 2)
-        out_ref[:, h * LATENT : (h + 1) * LATENT] = done[row : row + 1, :]
-
-
-def share_kernel(offsets, first_place, *refs):
-    *block_refs, out_ref, scores_ref, mask_ref = refs
+    done = mixed / total
+    tiles = LATENT // LANES
+    pair_count = HEADS // 2
+    for j in range(tiles):
+        part = done[:, j * LANES : (j + 1) * LANES]
+        flat_ref[pl.ds(j, pair_count, stride=2 * tiles), :] = part[:pair_count]
+        flat_ref[pl.ds(tiles + j, pair_count, stride=2 * tiles), :] = part[pair_count:]
+    out_ref[...] = flat_ref[...].reshape(out_ref.shape).astype(jnp.bfloat16)
+
+
+def log_share(offsets, first_place, block_refs, out_ref, scores_ref, mask_ref):
     shards, rows, keys_here = scores_ref.shape
     me = lax.axis_index("ctx")
     k = 0
@@ -263,6 +271,13 @@
     out_ref[...] = jnp.sum(jnp.where(diagonal, share, 0.0), axis=0, keepdims=True)
 
 
+def last_kernel(part_count, offsets, first_place, own_ref, lse_ref, *refs):
+    part_refs, block_refs = refs[:part_count], refs[part_count:-5]
+    out_ref, share_ref, flat_ref, scores_ref, mask_ref = refs[-5:]
+    combine(own_ref, lse_ref, part_refs, out_ref, flat_ref)
+    log_share(offsets, first_place, block_refs, share_ref, scores_ref, mask_ref)
+
+
 def body(att_query, latent_cache, index_query, index_weight, index_keys, selected):
     shards = lax.axis_size("ctx")
     blocks = lax.axis_size("pb")
@@ -273,55 +288,60 @@
 
     latent = latent_cache.T
     near = swap_apart(latent, 1, 2)
+    far = hold(swap_apart(near, 2, 1), 0)
 
     packed_rows = HEADS + round_up(max(shards, TAIL_ROWS), 16)
-    half_rows = row_width // 2
-    inputs = (selected[0], att_query[0], latent, index_query[0], index_weight[0], index_keys)
+    inputs = (selected[0], att_query[0], index_query[0], index_weight[0], index_keys)
     inputs = [pltpu.with_memory_space_constraint(x, pltpu.HBM) for x in inputs]
     held = [pltpu.VMEM(x.shape, x.dtype) for x in (selected[0], att_query[0], index_query[0], index_weight[0], index_keys)]
-    packed, half, share_own = call(
+    packed, share_own = call(
         prepare_kernel,
         (
             shape((packed_rows, LATENT), bf16),
-            shape((half_rows, keys_here), bf16),
             shape((rows + shards, keys_here), f32),
         ),
-        (*held, pltpu.SemaphoreType.DMA((6,)), pltpu.VMEM((HEADS // 2, 2 * row_width), f32)),
+        (*held, pltpu.SemaphoreType.DMA((5,)), pltpu.VMEM((HEADS * row_width // LANES, LANES), f32)),
         in_specs=[pl.BlockSpec(memory_space=pltpu.HBM)] * len(inputs),
     )(*inputs)
-    far_half = swap(half, 3)
-
-    near_other = swap_cores(near)
-    far_other = swap_cores(far_half)
-    span_rows = (latent, near, near_other, far_half, far_other)
-
-    scratch = (pltpu.VMEM((row_width, keys_here), bf16), pltpu.VMEM((packed_rows - HEADS, keys_here), f32))
+
+    near_other = hold(swap_cores(near), 0)
+    span_rows = (latent, near, near_other, far)
+
+    scratch = (pltpu.VMEM((packed_rows - HEADS, keys_here), f32),)
+    wide, narrow = shape((HEADS, LATENT), f32), shape((HEADS, LANES), f32)
     parts = []
     for k in range(1, shards // SPAN):
-        asked = hold(swap(packed, SPAN * k), 3000000000)
-        sent = call(send_kernel, shape((HEADS, LATENT + LANES), bf16), scratch)(asked, *span_rows)
-        parts.append(hold(swap(sent, SPAN * k), 10000000000))
-    kept, kept_lse = call(
-        keep_kernel, (shape((HEADS, LATENT), f32), shape((HEADS, LANES), f32)), scratch
-    )(packed, *span_rows)
-    attended = call(combine_kernel, shape((1, HEADS * LATENT), bf16))(kept, kept_lse, *parts)
+        asked = hold(swap(packed, SPAN * k), 100000000)
+        begun = call(
+            begin_kernel,
+            (wide, narrow, narrow),
+            scratch,
+            cost_estimate=pl.CostEstimate(flops=100000000, bytes_accessed=0, transcendentals=0),
+        )(asked, *span_rows[:3])
+        sent = call(send_kernel, shape((HEADS, LATENT + LANES), bf16), scratch)(asked, far, *begun)
+        parts.append(hold(swap(sent, SPAN * k), 0))
+    kept = call(keep_kernel, (wide, narrow), scratch)(packed, *span_rows)
 
     held, offsets = share_own[None], [0]
-    bits = [1 << b for b in range(2, shards.bit_length() - 1)] + [1, 2]
+    bits = [1 << b for b in range(2, shards.bit_length() - 1)] + [2, 1]
     arrived = held
     for step, bit in enumerate(bits):
         if step:
-            held = join(held, arrived, share_own if step < 2 else sent)
+            held = join(held, arrived, near if step < 2 else sent)
         arrived = swap(held, bit)
         if not step:
-            arrived = hold(arrived, 20000000000)
+            arrived = hold(arrived, 10000000000)
         offsets = offsets + [o ^ bit for o in offsets]
-    log_share = call(
-        functools.partial(share_kernel, offsets, keys_here * shards - rows * blocks),
-        shape((1, rows), f32),
-        (pltpu.VMEM((shards, rows, keys_here), f32), pltpu.VMEM((shards, shards, keys_here), f32)),
-    )(held, arrived)
-    return attended[None], log_share
+    attended, shares = call(
+        functools.partial(last_kernel, len(parts), offsets, keys_here * shards - rows * blocks),
+        (shape((1, HEADS * LATENT), bf16), shape((1, rows), f32)),
+        (
+            pltpu.VMEM((HEADS * LATENT // LANES, LANES), f32),
+            pltpu.VMEM((shards, rows, keys_here), f32),
+            pltpu.VMEM((shards, shards, keys_here), f32),
+        ),
+    )(*kept, *parts, held, arrived)
+    return attended[None], shares
 
 
 def solution(mesh):

time: 25.3 us -> 24.9 us (0.984)
    ppermute x6 -> x5, waiting for transfers between devices: 7.05 us -> 3.89 us  [swap(): return lax.ppermute(x, 'ctx', [(i, i ^ offset) for i in range(size)])]
    ppermute x1 -> x2, waiting for transfers between devices: 0.01 us -> 3.06 us  [swap_apart(): return lax.ppermute(x, ('ctx', 'pb'), moves)]
    ppermute x6 -> x5, starting transfers between devices: 9.64 us -> 7.34 us  [swap(): return lax.ppermute(x, 'ctx', [(i, i ^ offset) for i in range(size)])]
    ppermute x1 -> x2, starting transfers between devices: 3 us -> 5.11 us  [swap_apart(): return lax.ppermute(x, ('ctx', 'pb'), moves)]
    pallas_call x1, Pallas kernels: 0.84 us -> 0.52 us  [body(): call(send_kernel, shape((HEADS, LATENT + LANES), bf16), scratch)]
    pallas_call x7 -> x6, Pallas kernels: 3.92 us -> 4.09 us  [the longest x1 1.44 us: body(): call(prepare_kernel, (shape((packed_rows, LATENT), bf16), shape((rows + s...]
  transfers between devices with their start and end apart: 9 -> 8, of which waited for: 4 -> 4; matrix products, arithmetic and copies ran while one was open for 0% -> 0% of each run, Pallas kernels for 16% -> 15%
where the time goes in v3:
time: 24.9 us; the launch traced here: 24.7 us
  starting transfers between devices  12.5 us (50%)
  waiting for transfers between devices  6.95 us (28%)
  Pallas kernels  4.62 us (19%)
  between operations  0.67 us (3%)
    ppermute x5, starting transfers between devices, swap(): return lax.ppermute(x, 'ctx', [(i, i ^ offset) for i in range(size)])  7.34 us
    ppermute x2, starting transfers between devices, swap_apart(): return lax.ppermute(x, ('ctx', 'pb'), moves)  5.11 us
    ppermute x5, waiting for transfers between devices, swap(): return lax.ppermute(x, 'ctx', [(i, i ^ offset) for i in range(size)])  3.89 us
    ppermute x2, waiting for transfers between devices, swap_apart(): return lax.ppermute(x, ('ctx', 'pb'), moves)  3.06 us
    pallas_call x1, Pallas kernels, body(): call(prepare_kernel, (shape((packed_rows, LATENT), bf16), shape((rows + s...  1.44 us
    pallas_call x1, Pallas kernels, body(): call(functools.partial(last_kernel, len(parts), offsets, keys_here * shar...  1 us
    pallas_call x1, Pallas kernels, body(): kept = call(keep_kernel, (wide, narrow), scratch)(packed, *span_rows)  0.83 us
    pallas_call x1, Pallas kernels, body(): call(begin_kernel, (wide, narrow, narrow), scratch, cost_estimate=pl.Cost...  0.81 us
  transfers between devices with their start and end apart: 8, of which 4 were waited for; matrix products, arithmetic and copies ran while one was open for 0% of the time, Pallas kernels for 15%

profile of v3, /device:TPU:0, one launch (start us, length us, event | category | flops | bytes accessed | tf_op | source)
XLA Modules:
  0.0 24.7 jit_solution(7490673366819044269)
XLA Ops:
  0.6 3.0 %collective-permute-start = (bf16[576,256]{1,0:T(8,128)(2,1)}, bf16[576,256]{1,0:T(8,128)(2,1)S(1)}, u32[]{:S(2)}, u32[]{:S(2)}) collective-permute-start(bf16[576,256]{1,0:T(8,128)(2,1)} %bitcast.7), channel_id=1, source_target_pairs={{0,2},{1,5},{2,0},{3,7},{4,6},{5,1},{6,4},{7,3},{8,10},{9,13},{10,... | collective-permute-start | bytes 884744 | tf_op jit(solution)/shard_map/ppermute | solution.py:44
  3.6 1.4 %shard_map.77 = (bf16[80,512]{1,0:T(8,128)(2,1)S(1)}, f32[16,256]{1,0:T(8,128)S(1)}) custom-call(s32[1,1024]{1,0:T(1,128)} %bitcast.14, bf16[1,36864]{1,0:T(2,128)(2,1)} %bitcast.12, bf16[8,4096]{1,0:T(8,128)(2,1)} %bitcast.13, f32[8,32]{1,0:T(8,128)} %bitcast.15, bf16[256,128]{1,0:T(8,128)(2,1)} %keys_ref.1), custom_call_target="tpu_custom_call" | custom-call | tf_op jit(solution)/shard_map/pallas_call | solution.py:297
  5.1 2.7 %collective-permute-start.5 = (f32[1,16,256]{2,1,0:T(8,128)S(1)}, f32[1,16,256]{2,1,0:T(8,128)S(1)}, u32[]{:S(2)}, u32[]{:S(2)}) collective-permute-start(f32[1,16,256]{2,1,0:T(8,128)S(1)} %bitcast.10), channel_id=1, source_target_pairs={{0,8},{2,10},{4,12},{6,14},{8,0},{10,2},{12,4},{14,6},{1,9},{3,11}... | collective-permute-start | bytes 49160 | tf_op jit(solution)/shard_map/ppermute | solution.py:29
  7.7 0.3 %collective-permute-start.3 = (bf16[80,512]{1,0:T(8,128)(2,1)S(1)}, bf16[80,512]{1,0:T(8,128)(2,1)S(1)}, u32[]{:S(2)}, u32[]{:S(2)}) collective-permute-start(bf16[80,512]{1,0:T(8,128)(2,1)S(1)} %get-tuple-element.11.packed_ref), channel_id=1, source_target_pairs={{0,8},{2,10},{4,12},{6,14},{8,0},{10,2},{12,4},{14,6},{1,9},{3,11}... | collective-permute-start | bytes 245768 | tf_op jit(solution)/shard_map/ppermute | solution.py:29
  8.1 0.5 %collective-permute-done.first_ref.after_ref = bf16[576,256]{1,0:T(8,128)(2,1)S(1)} collective-permute-done((bf16[576,256]{1,0:T(8,128)(2,1)}, bf16[576,256]{1,0:T(8,128)(2,1)S(1)}, u32[]{:S(2)}, u32[]{:S(2)}) %collective-permute-start) | collective-permute-done | bytes 294944 | tf_op jit(solution)/shard_map/ppermute | solution.py:44
  8.6 0.0 collective-permute-start.1
  8.6 2.1 %collective-permute-start.2 = (bf16[576,256]{1,0:T(8,128)(2,1)S(1)}, bf16[576,256]{1,0:T(8,128)(2,1)S(1)}, u32[]{:S(2)}, u32[]{:S(2)}) collective-permute-start(bf16[576,256]{1,0:T(8,128)(2,1)S(1)} %collective-permute-done.first_ref.after_ref), channel_id=1, source_target_pairs={{0,4},{1,3},{2,6},{3,1},{4,0},{5,7},{6,2},{7,5},{8,12},{9,11},{10,... | collective-permute-start | bytes 884744 | tf_op jit(solution)/shard_map/ppermute | solution.py:44
  10.7 0.0 collective-permute-done.5.refs_0_
  10.7 0.0 copy-start
  10.7 0.9 %collective-permute-start.6 = (f32[2,16,256]{2,1,0:T(8,128)S(1)}, f32[2,16,256]{2,1,0:T(8,128)S(1)}, u32[]{:S(2)}, u32[]{:S(2)}) collective-permute-start(f32[2,16,256]{2,1,0:T(8,128)S(1)} %shard_map.83.left_ref), channel_id=1, source_target_pairs={{0,4},{2,6},{4,0},{6,2},{8,12},{10,14},{12,8},{14,10},{1,5},{3,7},... | collective-permute-start | bytes 98312 | tf_op jit(solution)/shard_map/ppermute | solution.py:29
  11.6 1.8 %collective-permute-done.3.refs_0_ = bf16[80,512]{1,0:T(8,128)(2,1)S(1)} collective-permute-done((bf16[80,512]{1,0:T(8,128)(2,1)S(1)}, bf16[80,512]{1,0:T(8,128)(2,1)S(1)}, u32[]{:S(2)}, u32[]{:S(2)}) %collective-permute-start.3) | collective-permute-done | bytes 81952 | tf_op jit(solution)/shard_map/ppermute | solution.py:29
  13.4 0.0 collective-permute-done.1.second_ref
  13.4 0.0 copy-done
  13.4 0.8 %shard_map.80 = (f32[64,512]{1,0:T(8,128)S(1)}, f32[64,128]{1,0:T(8,128)S(1)}, f32[64,128]{1,0:T(8,128)S(1)}) custom-call(bf16[80,512]{1,0:T(8,128)(2,1)S(1)} %shard_map.79.packed_ref, bf16[576,256]{1,0:T(8,128)(2,1)S(1)} %bitcast.8, bf16[576,256]{1,0:T(8,128)(2,1)S(1)} %collective-permute-done.first_ref.after_ref, ...), custom_call_target="tpu_custom_call" | custom-call | flops 100000000 | tf_op jit(solution)/shard_map/pallas_call | solution.py:315
  14.2 2.6 %collective-permute-done.2.far_ref = bf16[576,256]{1,0:T(8,128)(2,1)S(1)} collective-permute-done((bf16[576,256]{1,0:T(8,128)(2,1)S(1)}, bf16[576,256]{1,0:T(8,128)(2,1)S(1)}, u32[]{:S(2)}, u32[]{:S(2)}) %collective-permute-start.2) | collective-permute-done | bytes 294944 | tf_op jit(solution)/shard_map/ppermute | solution.py:44
  16.8 0.5 %shard_map.81.after_ref = bf16[64,640]{1,0:T(8,128)(2,1)S(1)} custom-call(bf16[80,512]{1,0:T(8,128)(2,1)S(1)} %shard_map.79.packed_ref, bf16[576,256]{1,0:T(8,128)(2,1)S(1)} %collective-permute-done.2.far_ref, f32[64,512]{1,0:T(8,128)S(1)} %get-tuple-element.14.mixed_ref, f32[64,128]{1,0:T(8,128)S(1)} %get-tuple-element.15.highest_ref, ...), custom_call_target="tpu_custom_call" | custom-call | tf_op jit(solution)/shard_map/pallas_call | solution.py:321
  17.3 2.0 %collective-permute-start.4 = (bf16[64,640]{1,0:T(8,128)(2,1)S(1)}, bf16[64,640]{1,0:T(8,128)(2,1)S(1)}, u32[]{:S(2)}, u32[]{:S(2)}) collective-permute-start(bf16[64,640]{1,0:T(8,128)(2,1)S(1)} %shard_map.81.after_ref), channel_id=1, source_target_pairs={{0,8},{2,10},{4,12},{6,14},{8,0},{10,2},{12,4},{14,6},{1,9},{3,11}... | collective-permute-start | bytes 245768 | tf_op jit(solution)/shard_map/ppermute | solution.py:29
  19.3 0.0 collective-permute-done.6.right_ref
  19.4 1.4 %collective-permute-start.7 = (f32[4,16,256]{2,1,0:T(8,128)S(1)}, f32[4,16,256]{2,1,0:T(8,128)S(1)}, u32[]{:S(2)}, u32[]{:S(2)}) collective-permute-start(f32[4,16,256]{2,1,0:T(8,128)S(1)} %shard_map.84.refs_1_), channel_id=1, source_target_pairs={{0,2},{2,0},{4,6},{6,4},{8,10},{10,8},{12,14},{14,12},{1,3},{3,1},... | collective-permute-start | bytes 196616 | tf_op jit(solution)/shard_map/ppermute | solution.py:29
  20.8 0.8 %shard_map.78 = (f32[64,512]{1,0:T(8,128)S(1)}, f32[64,128]{1,0:T(8,128)S(1)}) custom-call(bf16[80,512]{1,0:T(8,128)(2,1)S(1)} %get-tuple-element.11.packed_ref, bf16[576,256]{1,0:T(8,128)(2,1)S(1)} %bitcast.9, bf16[576,256]{1,0:T(8,128)(2,1)S(1)} %collective-permute-done.first_ref.after_ref, bf16[576,256]{1,0:T(8,128)(2,1)S(1)} %collective-permute-done.1.second_ref, ...), custom_call_target="tpu_custom_call" | custom-call | tf_op jit(solution)/shard_map/pallas_call | solution.py:323
  21.6 2.1 %collective-permute-done.7.refs_2_ = f32[4,16,256]{2,1,0:T(8,128)S(1)} collective-permute-done((f32[4,16,256]{2,1,0:T(8,128)S(1)}, f32[4,16,256]{2,1,0:T(8,128)S(1)}, u32[]{:S(2)}, u32[]{:S(2)}) %collective-permute-start.7) | collective-permute-done | bytes 65568 | tf_op jit(solution)/shard_map/ppermute | solution.py:29
  23.7 0.0 collective-permute-done.4.refs_0_
  23.7 1.0 %shard_map.85 = (bf16[1,32768]{1,0:T(2,128)(2,1)}, f32[1,8]{1,0:T(1,128)}) custom-call(f32[64,512]{1,0:T(8,128)S(1)} %get-tuple-element.12.own_ref, f32[64,128]{1,0:T(8,128)S(1)} %get-tuple-element.13.lse_ref, bf16[64,640]{1,0:T(8,128)(2,1)S(1)} %collective-permute-done.4.refs_0_, f32[4,16,256]{2,1,0:T(8,128)S(1)} %shard_map.84.refs_1_, ...), custom_call_target="tpu_custom_call" | custom-call | tf_op jit(solution)/shard_map/pallas_call | solution.py:335
  (4 shorter events, 0.0 us)
Async XLA Ops:
  0.6 7.9 %collective-permute-start = (bf16[576,256]{1,0:T(8,128)(2,1)}, bf16[576,256]{1,0:T(8,128)(2,1)S(1)}, u32[]{:S(2)}, u32[]{:S(2)}) collective-permute-start(bf16[576,256]{1,0:T(8,128)(2,1)} %bitcast.7), channel_id=1, source_target_pairs={{0,2},{1,5},{2,0},{3,7},{4,6},{5,1},{6,4},{7,3},{8,10},{9,13},{10,... | collective-permute-start | bytes 884744 | tf_op jit(solution)/shard_map/ppermute | solution.py:44
  5.1 5.6 %collective-permute-start.5 = (f32[1,16,256]{2,1,0:T(8,128)S(1)}, f32[1,16,256]{2,1,0:T(8,128)S(1)}, u32[]{:S(2)}, u32[]{:S(2)}) collective-permute-start(f32[1,16,256]{2,1,0:T(8,128)S(1)} %bitcast.10), channel_id=1, source_target_pairs={{0,8},{2,10},{4,12},{6,14},{8,0},{10,2},{12,4},{14,6},{1,9},{3,11}... | collective-permute-start | bytes 49160 | tf_op jit(solution)/shard_map/ppermute | solution.py:29
  7.7 5.7 %collective-permute-start.3 = (bf16[80,512]{1,0:T(8,128)(2,1)S(1)}, bf16[80,512]{1,0:T(8,128)(2,1)S(1)}, u32[]{:S(2)}, u32[]{:S(2)}) collective-permute-start(bf16[80,512]{1,0:T(8,128)(2,1)S(1)} %get-tuple-element.11.packed_ref), channel_id=1, source_target_pairs={{0,8},{2,10},{4,12},{6,14},{8,0},{10,2},{12,4},{14,6},{1,9},{3,11}... | collective-permute-start | bytes 245768 | tf_op jit(solution)/shard_map/ppermute | solution.py:29
  8.6 4.8 %collective-permute-start.1 = (bf16[576,256]{1,0:T(8,128)(2,1)S(1)}, bf16[576,256]{1,0:T(8,128)(2,1)S(1)}, u32[]{:S(2)}, u32[]{:S(2)}) collective-permute-start(bf16[576,256]{1,0:T(8,128)(2,1)S(1)} %collective-permute-done.first_ref.after_ref), channel_id=1, source_target_pairs={{0,1},{1,0},{2,3},{3,2},{4,5},{5,4},{6,7},{7,6},{8,9},{9,8},{10,11... | collective-permute-start | bytes 884744 | tf_op jit(solution)/shard_map/ppermute | solution.py:34
  8.6 8.2 %collective-permute-start.2 = (bf16[576,256]{1,0:T(8,128)(2,1)S(1)}, bf16[576,256]{1,0:T(8,128)(2,1)S(1)}, u32[]{:S(2)}, u32[]{:S(2)}) collective-permute-start(bf16[576,256]{1,0:T(8,128)(2,1)S(1)} %collective-permute-done.first_ref.after_ref), channel_id=1, source_target_pairs={{0,4},{1,3},{2,6},{3,1},{4,0},{5,7},{6,2},{7,5},{8,12},{9,11},{10,... | collective-permute-start | bytes 884744 | tf_op jit(solution)/shard_map/ppermute | solution.py:44
  10.7 2.7 %copy-start = (bf16[256,576]{0,1:T(8,128)(2,1)S(1)}, bf16[256,576]{0,1:T(8,128)(2,1)}, u32[]{:S(2)}) copy-start(bf16[256,576]{0,1:T(8,128)(2,1)} %param.7) | copy-start | bytes 884740
  10.7 8.7 %collective-permute-start.6 = (f32[2,16,256]{2,1,0:T(8,128)S(1)}, f32[2,16,256]{2,1,0:T(8,128)S(1)}, u32[]{:S(2)}, u32[]{:S(2)}) collective-permute-start(f32[2,16,256]{2,1,0:T(8,128)S(1)} %shard_map.83.left_ref), channel_id=1, source_target_pairs={{0,4},{2,6},{4,0},{6,2},{8,12},{10,14},{12,8},{14,10},{1,5},{3,7},... | collective-permute-start | bytes 98312 | tf_op jit(solution)/shard_map/ppermute | solution.py:29
  17.3 6.4 %collective-permute-start.4 = (bf16[64,640]{1,0:T(8,128)(2,1)S(1)}, bf16[64,640]{1,0:T(8,128)(2,1)S(1)}, u32[]{:S(2)}, u32[]{:S(2)}) collective-permute-start(bf16[64,640]{1,0:T(8,128)(2,1)S(1)} %shard_map.81.after_ref), channel_id=1, source_target_pairs={{0,8},{2,10},{4,12},{6,14},{8,0},{10,2},{12,4},{14,6},{1,9},{3,11}... | collective-permute-start | bytes 245768 | tf_op jit(solution)/shard_map/ppermute | solution.py:29
  19.4 4.3 %collective-permute-start.7 = (f32[4,16,256]{2,1,0:T(8,128)S(1)}, f32[4,16,256]{2,1,0:T(8,128)S(1)}, u32[]{:S(2)}, u32[]{:S(2)}) collective-permute-start(f32[4,16,256]{2,1,0:T(8,128)S(1)} %shard_map.84.refs_1_), channel_id=1, source_target_pairs={{0,2},{2,0},{4,6},{6,4},{8,10},{10,8},{12,14},{14,12},{1,3},{3,1},... | collective-permute-start | bytes 196616 | tf_op jit(solution)/shard_map/ppermute | solution.py:29

commit v4 on v3

--- a/solution.py
+++ b/solution.py
@@ -201,11 +201,15 @@
     scale, far_scale = jnp.exp(highest_ref[:, :1] - highest), jnp.exp(far_highest - highest)
     total = total_ref[:, :1] * scale + far_total * far_scale
     mixed, lse = finish(mixed_ref[...] * scale + far_mixed * far_scale, highest, total)
-    high, middle, low = split(lse)
-    lane = lax.broadcasted_iota(jnp.int32, (HEADS, LANES), 1)
-    tail = jnp.where(lane == 0, high, jnp.where(lane == 1, middle, low))
-    out_ref[:, :LATENT] = mixed.astype(jnp.bfloat16)
-    out_ref[:, LATENT:] = tail.astype(jnp.bfloat16)
+    for j in range(LATENT // LANES):
+        out_ref[j * HEADS : (j + 1) * HEADS, :] = mixed[:, j * LANES : (j + 1) * LANES].astype(jnp.bfloat16)
+    logs = [jnp.sum(jnp.where(head_lanes(), part, 0.0), axis=0, keepdims=True) for part in split(lse)]
+    out_ref[HEADS * LATENT // LANES :, :] = padded(jnp.concatenate(logs, axis=0), TAIL_ROWS).astype(jnp.bfloat16)
+
+
+def head_lanes():
+    shape = (HEADS, LANES)
+    return lax.broadcasted_iota(jnp.int32, shape, 0) == lax.broadcasted_iota(jnp.int32, shape, 1)
 
 
 def keep_kernel(packed_ref, own_ref, first_ref, second_ref, far_ref, out_ref, lse_ref, mask_ref):
@@ -223,9 +227,14 @@
 def combine(own_ref, lse_ref, part_refs, out_ref, flat_ref):
     mixes, lses = [own_ref[...]], [lse_ref[:, :1]]
     for ref in part_refs:
-        tail = ref[:, LATENT:].astype(jnp.float32)
-        lses.append(tail[:, 0:1] + tail[:, 1:2] + tail[:, 2:3])
-        mixes.append(ref[:, :LATENT].astype(jnp.float32))
+        logs = ref[HEADS * LATENT // LANES :, :].astype(jnp.float32)
+        log = logs[0:1] + logs[1:2] + logs[2:3]
+        lses.append(jnp.sum(jnp.where(head_lanes(), log, 0.0), axis=1, keepdims=True))
+        mixes.append(
+            jnp.concatenate(
+                [ref[j * HEADS : (j + 1) * HEADS, :].astype(jnp.float32) for j in range(LATENT // LANES)], axis=1
+            )
+        )
     peak = functools.reduce(jnp.maximum, lses)
     weights = [jnp.exp(lse - peak) for lse in lses]
     total = functools.reduce(jnp.add, weights)
@@ -240,42 +249,87 @@
     out_ref[...] = flat_ref[...].reshape(out_ref.shape).astype(jnp.bfloat16)
 
 
-def log_share(offsets, first_place, block_refs, out_ref, scores_ref, mask_ref):
-    shards, rows, keys_here = scores_ref.shape
+def fold_kernel(offsets, bit, first_place, left_ref, right_ref, out_ref, keep_ref):
+    count = len(offsets)
+    half = left_ref.shape[0]
+    rows, keys_here = keep_ref.shape[1:]
     me = lax.axis_index("ctx")
-    k = 0
-    for ref in block_refs:
-        for j in range(ref.shape[0]):
-            owner = me ^ offsets[k]
-            scores_ref[owner] = ref[j, :rows, :]
-            mask_ref[owner] = ref[j, rows:, :]
-            k += 1
+    owners = [me ^ offset for offset in offsets]
+    blocks = [left_ref.at[j] for j in range(half)] + [right_ref.at[j] for j in range(count - half)]
+    keep_ref[...] = jnp.zeros(keep_ref.shape, jnp.float32)
+    for k in range(count):
+        for t in range(count):
+            row = k * count + t
+            out_ref[row : row + 1, :] = blocks[k][pl.ds(rows + (owners[t] ^ bit), 1), :]
+            row += count * count
+            out_ref[row : row + 1, :] = blocks[t][pl.ds(owners[k] ^ bit, 1), :]
+            keep_ref[t, pl.ds(owners[k], 1), :] = blocks[k][pl.ds(rows + owners[t], 1), :]
     start = first_place + lax.axis_index("pb") * rows
     query_place = start + lax.broadcasted_iota(jnp.int32, (rows, keys_here), 0)
     key_place = lax.broadcasted_iota(jnp.int32, (rows, keys_here), 1)
-    causal = [key_place + t * keys_here <= query_place for t in range(shards)]
-    chosen = [mask_ref[:, t, :] > 0.5 for t in range(shards)]
-
-    def lse(keeps):
+    scores = [block[:rows, :] for block in blocks]
+    causal = [key_place + owner * keys_here <= query_place for owner in owners]
+    chosen = [keep_ref[t] > 0.5 for t in range(count)]
+    lane = lax.broadcasted_iota(jnp.int32, (rows, keys_here), 1)
+    tail = jnp.zeros((rows, keys_here), jnp.float32)
+    for place, keeps in enumerate((causal, chosen)):
         peak = jnp.full((rows, keys_here), floor_value, jnp.float32)
-        for t in range(shards):
-            peak = jnp.maximum(peak, jnp.where(keeps[t], scores_ref[t], floor_value))
+        for t in range(count):
+            peak = jnp.maximum(peak, jnp.where(keeps[t], scores[t], floor_value))
         peak = jnp.max(peak, axis=1, keepdims=True)
         total = jnp.zeros((rows, keys_here), jnp.float32)
-        for t in range(shards):
-            total += jnp.where(keeps[t], jnp.exp(scores_ref[t] - peak), 0.0)
-        return peak + jnp.log(jnp.sum(total, axis=1, keepdims=True))
-
-    share = lse(chosen) - lse(causal)
-    diagonal = lax.broadcasted_iota(jnp.int32, (rows, rows), 0) == lax.broadcasted_iota(jnp.int32, (rows, rows), 1)
-    out_ref[...] = jnp.sum(jnp.where(diagonal, share, 0.0), axis=0, keepdims=True)
-
-
-def last_kernel(part_count, offsets, first_place, own_ref, lse_ref, *refs):
-    part_refs, block_refs = refs[:part_count], refs[part_count:-5]
-    out_ref, share_ref, flat_ref, scores_ref, mask_ref = refs[-5:]
+        for t in range(count):
+            total += jnp.where(keeps[t], jnp.exp(scores[t] - peak), 0.0)
+        total = jnp.sum(total, axis=1, keepdims=True)
+        tail = jnp.where(lane == 2 * place, peak, jnp.where(lane == 2 * place + 1, total, tail))
+    out_ref[2 * count * count :, :] = tail
+
+
+def log_share(offsets, bit, here_ref, there_ref, out_ref):
+    count = len(offsets)
+    cross = count * count
+    rows = out_ref.shape[1]
+    me = lax.axis_index("ctx")
+    row = lax.broadcasted_iota(jnp.int32, (cross, LANES), 0)
+    lane = lax.broadcasted_iota(jnp.int32, (cross, LANES), 1)
+    query = jnp.zeros((cross, LANES), jnp.int32)
+    for k in range(count):
+        query = jnp.where(row // count == k, me ^ offsets[k], query)
+
+    def pieces(mask_ref, score_ref, query):
+        keep = mask_ref[:cross, :] > 0.5
+        scores = score_ref[cross : 2 * cross, :]
+        peak = jnp.max(jnp.where(keep, scores, floor_value), axis=1, keepdims=True)
+        total = jnp.sum(jnp.where(keep, jnp.exp(scores - peak), 0.0), axis=1, keepdims=True)
+        return peak, total, query == lane
+
+    def sides(place):
+        found = []
+        for ref in (here_ref, there_ref):
+            tail = ref[2 * cross :, :]
+            mine = lax.broadcasted_iota(jnp.int32, (rows, LANES), 0) == lax.broadcasted_iota(jnp.int32, (rows, LANES), 1)
+            found.append((tail[:, 2 * place : 2 * place + 1], tail[:, 2 * place + 1 : 2 * place + 2], mine))
+        return found
+
+    def lse(parts):
+        peaks = [jnp.max(jnp.where(mine, peak, floor_value), axis=0, keepdims=True) for peak, _, mine in parts]
+        highest = functools.reduce(jnp.maximum, peaks)
+        totals = [
+            jnp.sum(jnp.where(mine, total * jnp.exp(jnp.where(mine, peak - highest, 0.0)), 0.0), axis=0, keepdims=True)
+            for peak, total, mine in parts
+        ]
+        return highest + jnp.log(functools.reduce(jnp.add, totals))
+
+    across = [pieces(here_ref, there_ref, query), pieces(there_ref, here_ref, query ^ bit)]
+    share = lse(sides(1) + across) - lse(sides(0))
+    out_ref[...] = share[:, :rows]
+
+
+def last_kernel(part_count, offsets, bit, own_ref, lse_ref, *refs):
+    part_refs, (here_ref, there_ref) = refs[:part_count], refs[part_count : part_count + 2]
+    out_ref, share_ref, flat_ref = refs[part_count + 2 :]
     combine(own_ref, lse_ref, part_refs, out_ref, flat_ref)
-    log_share(offsets, first_place, block_refs, share_ref, scores_ref, mask_ref)
+    log_share(offsets, bit, here_ref, there_ref, share_ref)
 
 
 def body(att_query, latent_cache, index_query, index_weight, index_keys, selected):
@@ -288,7 +342,6 @@
 
     latent = latent_cache.T
     near = swap_apart(latent, 1, 2)
-    far = hold(swap_apart(near, 2, 1), 0)
 
     packed_rows = HEADS + round_up(max(shards, TAIL_ROWS), 16)
     inputs = (selected[0], att_query[0], index_query[0], index_weight[0], index_keys)
@@ -304,43 +357,50 @@
         in_specs=[pl.BlockSpec(memory_space=pltpu.HBM)] * len(inputs),
     )(*inputs)
 
+    near = hold(near, 0, packed)
+    far = hold(swap_apart(near, 2, 1), 0)
     near_other = hold(swap_cores(near), 0)
-    span_rows = (latent, near, near_other, far)
-
+    span_rows = (latent, near, near_other)
+
+    held, offsets = share_own[None], [0]
+    bits = [1 << b for b in range(2, shards.bit_length() - 1)] + [1, 2]
+    arrived = held
+    for step, bit in enumerate(bits[:-1]):
+        if step:
+            held = join(held, arrived, near_other)
+        arrived = swap(held, bit)
+        if not step:
+            arrived = hold(arrived, 10000000000)
+        offsets = offsets + [o ^ bit for o in offsets]
+    bit = bits[-1]
+    here = call(
+        functools.partial(fold_kernel, offsets, bit, keys_here * shards - rows * blocks),
+        shape((2 * len(offsets) ** 2 + rows, keys_here), f32),
+        (pltpu.VMEM((len(offsets), rows, keys_here), f32),),
+        in_specs=[pl.BlockSpec(memory_space=pltpu.VMEM)] * 2,
+    )(held, arrived)
+    there = swap(here, bit)
     scratch = (pltpu.VMEM((packed_rows - HEADS, keys_here), f32),)
     wide, narrow = shape((HEADS, LATENT), f32), shape((HEADS, LANES), f32)
+    far = hold(far, 0, here)
     parts = []
     for k in range(1, shards // SPAN):
-        asked = hold(swap(packed, SPAN * k), 100000000)
+        asked = hold(swap(packed, SPAN * k), 100000000, held)
         begun = call(
             begin_kernel,
             (wide, narrow, narrow),
             scratch,
             cost_estimate=pl.CostEstimate(flops=100000000, bytes_accessed=0, transcendentals=0),
-        )(asked, *span_rows[:3])
-        sent = call(send_kernel, shape((HEADS, LATENT + LANES), bf16), scratch)(asked, far, *begun)
+        )(asked, *span_rows)
+        sent = call(send_kernel, shape((HEADS * LATENT // LANES + TAIL_ROWS, LANES), bf16), scratch)(asked, far, *begun)
         parts.append(hold(swap(sent, SPAN * k), 0))
-    kept = call(keep_kernel, (wide, narrow), scratch)(packed, *span_rows)
-
-    held, offsets = share_own[None], [0]
-    bits = [1 << b for b in range(2, shards.bit_length() - 1)] + [2, 1]
-    arrived = held
-    for step, bit in enumerate(bits):
-        if step:
-            held = join(held, arrived, near if step < 2 else sent)
-        arrived = swap(held, bit)
-        if not step:
-            arrived = hold(arrived, 10000000000)
-        offsets = offsets + [o ^ bit for o in offsets]
+    kept = call(keep_kernel, (wide, narrow), scratch)(packed, *span_rows, far)
+
     attended, shares = call(
-        functools.partial(last_kernel, len(parts), offsets, keys_here * shards - rows * blocks),
+        functools.partial(last_kernel, len(parts), offsets, bit),
         (shape((1, HEADS * LATENT), bf16), shape((1, rows), f32)),
-        (
-            pltpu.VMEM((HEADS * LATENT // LANES, LANES), f32),
-            pltpu.VMEM((shards, rows, keys_here), f32),
-            pltpu.VMEM((shards, shards, keys_here), f32),
-        ),
-    )(*kept, *parts, held, arrived)
+        (pltpu.VMEM((HEADS * LATENT // LANES, LANES), f32),),
+    )(*kept, *parts, here, there)
     return attended[None], shares
 
 

time: 24.9 us -> 24.7 us (level)
  waiting for transfers between devices: 6.95 us -> 5.75 us
  starting transfers between devices: 12.5 us -> 13.3 us
    ppermute x2, waiting for transfers between devices: 3.06 us -> 1.63 us  [swap_apart(): return lax.ppermute(x, ('ctx', 'pb'), moves)]
    ppermute x5, starting transfers between devices: 7.34 us -> 8.17 us  [swap(): return lax.ppermute(x, 'ctx', [(i, i ^ offset) for i in range(size)])]
    pallas_call x3 -> x4, Pallas kernels: 2.36 us -> 2.52 us  [the longest x1 0.95 us: body(): call(functools.partial(last_kernel, len(parts), offsets, bit), (shape((1,...]
  transfers between devices with their start and end apart: 8 -> 8, of which waited for: 4 -> 6; matrix products, arithmetic and copies ran while one was open for 0% -> 0% of each run, Pallas kernels for 15% -> 13%
where the time goes in v4:
time: 24.7 us; the launch traced here: 24.5 us
  starting transfers between devices  13.3 us (54%)
  waiting for transfers between devices  5.75 us (23%)
  Pallas kernels  4.78 us (19%)
  between operations  0.68 us (3%)
    ppermute x5, starting transfers between devices, swap(): return lax.ppermute(x, 'ctx', [(i, i ^ offset) for i in range(size)])  8.17 us
    ppermute x2, starting transfers between devices, swap_apart(): return lax.ppermute(x, ('ctx', 'pb'), moves)  5.11 us
    ppermute x5, waiting for transfers between devices, swap(): return lax.ppermute(x, 'ctx', [(i, i ^ offset) for i in range(size)])  4.13 us
    ppermute x2, waiting for transfers between devices, swap_apart(): return lax.ppermute(x, ('ctx', 'pb'), moves)  1.63 us
    pallas_call x1, Pallas kernels, body(): call(prepare_kernel, (shape((packed_rows, LATENT), bf16), shape((rows + s...  1.44 us
    pallas_call x1, Pallas kernels, body(): call(functools.partial(last_kernel, len(parts), offsets, bit), (shape((1,...  0.95 us
    pallas_call x1, Pallas kernels, body(): kept = call(keep_kernel, (wide, narrow), scratch)(packed, *span_rows, far)  0.83 us
    pallas_call x1, Pallas kernels, body(): call(begin_kernel, (wide, narrow, narrow), scratch, cost_estimate=pl.Cost...  0.82 us
  transfers between devices with their start and end apart: 8, of which 6 were waited for; matrix products, arithmetic and copies ran while one was open for 0% of the time, Pallas kernels for 13%

profile of v4, /device:TPU:0, one launch (start us, length us, event | category | flops | bytes accessed | tf_op | source)
XLA Modules:
  0.0 24.5 jit_solution(8038998248311794172)
XLA Ops:
  0.6 3.0 %collective-permute-start = (bf16[576,256]{1,0:T(8,128)(2,1)}, bf16[576,256]{1,0:T(8,128)(2,1)S(1)}, u32[]{:S(2)}, u32[]{:S(2)}) collective-permute-start(bf16[576,256]{1,0:T(8,128)(2,1)} %bitcast.7), channel_id=1, source_target_pairs={{0,2},{1,5},{2,0},{3,7},{4,6},{5,1},{6,4},{7,3},{8,10},{9,13},{10,... | collective-permute-start | bytes 884744 | tf_op jit(solution)/shard_map/ppermute | solution.py:44
  3.6 1.4 %shard_map.77 = (bf16[80,512]{1,0:T(8,128)(2,1)S(1)}, f32[16,256]{1,0:T(8,128)S(1)}) custom-call(s32[1,1024]{1,0:T(1,128)} %bitcast.14, bf16[1,36864]{1,0:T(2,128)(2,1)} %bitcast.12, bf16[8,4096]{1,0:T(8,128)(2,1)} %bitcast.13, f32[8,32]{1,0:T(8,128)} %bitcast.15, bf16[256,128]{1,0:T(8,128)(2,1)} %keys_ref.1), custom_call_target="tpu_custom_call" | custom-call | tf_op jit(solution)/shard_map/pallas_call | solution.py:350
  5.1 2.7 %collective-permute-start.3 = (f32[1,16,256]{2,1,0:T(8,128)S(1)}, f32[1,16,256]{2,1,0:T(8,128)S(1)}, u32[]{:S(2)}, u32[]{:S(2)}) collective-permute-start(f32[1,16,256]{2,1,0:T(8,128)S(1)} %bitcast.10), channel_id=1, source_target_pairs={{0,8},{2,10},{4,12},{6,14},{8,0},{10,2},{12,4},{14,6},{1,9},{3,11}... | collective-permute-start | bytes 49160 | tf_op jit(solution)/shard_map/ppermute | solution.py:29
  7.7 0.3 %collective-permute-start.5 = (bf16[80,512]{1,0:T(8,128)(2,1)S(1)}, bf16[80,512]{1,0:T(8,128)(2,1)S(1)}, u32[]{:S(2)}, u32[]{:S(2)}) collective-permute-start(bf16[80,512]{1,0:T(8,128)(2,1)S(1)} %get-tuple-element.11.refs_1_.packed_ref), channel_id=1, source_target_pairs={{0,8},{2,10},{4,12},{6,14},{8,0},{10,2},{12,4},{14,6},{1,9},{3,11}... | collective-permute-start | bytes 245768 | tf_op jit(solution)/shard_map/ppermute | solution.py:29
  8.1 0.5 %collective-permute-done.refs_0_ = bf16[576,256]{1,0:T(8,128)(2,1)S(1)} collective-permute-done((bf16[576,256]{1,0:T(8,128)(2,1)}, bf16[576,256]{1,0:T(8,128)(2,1)S(1)}, u32[]{:S(2)}, u32[]{:S(2)}) %collective-permute-start) | collective-permute-done | bytes 294944 | tf_op jit(solution)/shard_map/ppermute | solution.py:44
  8.6 0.0 collective-permute-start.1
  8.6 2.1 %collective-permute-start.2 = (bf16[576,256]{1,0:T(8,128)(2,1)S(1)}, bf16[576,256]{1,0:T(8,128)(2,1)S(1)}, u32[]{:S(2)}, u32[]{:S(2)}) collective-permute-start(bf16[576,256]{1,0:T(8,128)(2,1)S(1)} %shard_map.78.first_ref), channel_id=1, source_target_pairs={{0,4},{1,3},{2,6},{3,1},{4,0},{5,7},{6,2},{7,5},{8,12},{9,11},{10,... | collective-permute-start | bytes 884744 | tf_op jit(solution)/shard_map/ppermute | solution.py:44
  10.7 0.0 collective-permute-done.3.refs_0_
  10.7 0.0 copy-start
  10.7 0.0 collective-permute-done.1.after_ref.second_ref
  10.7 1.6 %collective-permute-start.4 = (f32[2,16,256]{2,1,0:T(8,128)S(1)}, f32[2,16,256]{2,1,0:T(8,128)S(1)}, u32[]{:S(2)}, u32[]{:S(2)}) collective-permute-start(f32[2,16,256]{2,1,0:T(8,128)S(1)} %shard_map.80.left_ref.refs_1_), channel_id=1, source_target_pairs={{0,2},{2,0},{4,6},{6,4},{8,10},{10,8},{12,14},{14,12},{1,3},{3,1},... | collective-permute-start | bytes 98312 | tf_op jit(solution)/shard_map/ppermute | solution.py:29
  12.2 1.1 %collective-permute-done.5.refs_0_ = bf16[80,512]{1,0:T(8,128)(2,1)S(1)} collective-permute-done((bf16[80,512]{1,0:T(8,128)(2,1)S(1)}, bf16[80,512]{1,0:T(8,128)(2,1)S(1)}, u32[]{:S(2)}, u32[]{:S(2)}) %collective-permute-start.5) | collective-permute-done | bytes 81952 | tf_op jit(solution)/shard_map/ppermute | solution.py:29
  13.4 0.0 copy-done
  13.4 0.8 %shard_map.85 = (f32[64,512]{1,0:T(8,128)S(1)}, f32[64,128]{1,0:T(8,128)S(1)}, f32[64,128]{1,0:T(8,128)S(1)}) custom-call(bf16[80,512]{1,0:T(8,128)(2,1)S(1)} %shard_map.84.packed_ref, bf16[576,256]{1,0:T(8,128)(2,1)S(1)} %bitcast.8, bf16[576,256]{1,0:T(8,128)(2,1)S(1)} %shard_map.78.first_ref, bf16[576,256]{1,0:T(8,128)(2,1)S(1)} %collective-permute-done.1.after_ref.second_ref), custom_call_target="tpu_custom_call" | custom-call | flops 100000000 | tf_op jit(solution)/shard_map/pallas_call | solution.py:389
  14.2 0.9 %collective-permute-done.4.right_ref = f32[2,16,256]{2,1,0:T(8,128)S(1)} collective-permute-done((f32[2,16,256]{2,1,0:T(8,128)S(1)}, f32[2,16,256]{2,1,0:T(8,128)S(1)}, u32[]{:S(2)}, u32[]{:S(2)}) %collective-permute-start.4) | collective-permute-done | bytes 32800 | tf_op jit(solution)/shard_map/ppermute | solution.py:29
  15.1 0.2 shard_map.81.refs_1_
  15.3 1.1 %collective-permute-done.2.refs_0_ = bf16[576,256]{1,0:T(8,128)(2,1)S(1)} collective-permute-done((bf16[576,256]{1,0:T(8,128)(2,1)S(1)}, bf16[576,256]{1,0:T(8,128)(2,1)S(1)}, u32[]{:S(2)}, u32[]{:S(2)}) %collective-permute-start.2) | collective-permute-done | bytes 294944 | tf_op jit(solution)/shard_map/ppermute | solution.py:44
  16.4 0.5 %shard_map.86 = bf16[272,128]{1,0:T(8,128)(2,1)S(1)} custom-call(bf16[80,512]{1,0:T(8,128)(2,1)S(1)} %shard_map.84.packed_ref, bf16[576,256]{1,0:T(8,128)(2,1)S(1)} %shard_map.82.far_ref, f32[64,512]{1,0:T(8,128)S(1)} %get-tuple-element.15.mixed_ref, f32[64,128]{1,0:T(8,128)S(1)} %get-tuple-element.16.highest_ref, f32[64,128]{1,0:T(8,128)S(1)} %get-tuple-element.17.total_ref), custom_call_target="tpu_custom_call" | custom-call | tf_op jit(solution)/shard_map/pallas_call | solution.py:395
  17.0 2.0 %collective-permute-start.6 = (bf16[272,128]{1,0:T(8,128)(2,1)S(1)}, bf16[272,128]{1,0:T(8,128)(2,1)S(1)}, u32[]{:S(2)}, u32[]{:S(2)}) collective-permute-start(bf16[272,128]{1,0:T(8,128)(2,1)S(1)} %shard_map.86), channel_id=1, source_target_pairs={{0,8},{2,10},{4,12},{6,14},{8,0},{10,2},{12,4},{14,6},{1,9},{3,11}... | collective-permute-start | bytes 208904 | tf_op jit(solution)/shard_map/ppermute | solution.py:29
  19.0 1.6 %collective-permute-start.7 = (f32[40,256]{1,0:T(8,128)S(1)}, f32[40,256]{1,0:T(8,128)S(1)}, u32[]{:S(2)}, u32[]{:S(2)}) collective-permute-start(f32[40,256]{1,0:T(8,128)S(1)} %shard_map.81.refs_1_), channel_id=1, source_target_pairs={{0,4},{2,6},{4,0},{6,2},{8,12},{10,14},{12,8},{14,10},{1,5},{3,7},... | collective-permute-start | bytes 122888 | tf_op jit(solution)/shard_map/ppermute | solution.py:29
  20.6 0.8 %shard_map.83 = (f32[64,512]{1,0:T(8,128)S(1)}, f32[64,128]{1,0:T(8,128)S(1)}) custom-call(bf16[80,512]{1,0:T(8,128)(2,1)S(1)} %get-tuple-element.11.refs_1_.packed_ref, bf16[576,256]{1,0:T(8,128)(2,1)S(1)} %bitcast.9, bf16[576,256]{1,0:T(8,128)(2,1)S(1)} %shard_map.78.first_ref, bf16[576,256]{1,0:T(8,128)(2,1)S(1)} %collective-permute-done.1.after_ref.second_ref, ...), custom_call_target="tpu_custom_call" | custom-call | tf_op jit(solution)/shard_map/pallas_call | solution.py:397
  21.4 1.8 %collective-permute-done.7.refs_2_ = f32[40,256]{1,0:T(8,128)S(1)} collective-permute-done((f32[40,256]{1,0:T(8,128)S(1)}, f32[40,256]{1,0:T(8,128)S(1)}, u32[]{:S(2)}, u32[]{:S(2)}) %collective-permute-start.7) | collective-permute-done | bytes 40992 | tf_op jit(solution)/shard_map/ppermute | solution.py:29
  23.2 0.3 %collective-permute-done.6.refs_0_ = bf16[272,128]{1,0:T(8,128)(2,1)S(1)} collective-permute-done((bf16[272,128]{1,0:T(8,128)(2,1)S(1)}, bf16[272,128]{1,0:T(8,128)(2,1)S(1)}, u32[]{:S(2)}, u32[]{:S(2)}) %collective-permute-start.6) | collective-permute-done | bytes 69664 | tf_op jit(solution)/shard_map/ppermute | solution.py:29
  23.5 0.9 %shard_map.87 = (bf16[1,32768]{1,0:T(2,128)(2,1)}, f32[1,8]{1,0:T(1,128)}) custom-call(f32[64,512]{1,0:T(8,128)S(1)} %get-tuple-element.13.own_ref, f32[64,128]{1,0:T(8,128)S(1)} %get-tuple-element.14.lse_ref, bf16[272,128]{1,0:T(8,128)(2,1)S(1)} %collective-permute-done.6.refs_0_, f32[40,256]{1,0:T(8,128)S(1)} %shard_map.81.refs_1_, ...), custom_call_target="tpu_custom_call" | custom-call | tf_op jit(solution)/shard_map/pallas_call | solution.py:399
  (5 shorter events, 0.0 us)
Async XLA Ops:
  0.6 7.9 %collective-permute-start = (bf16[576,256]{1,0:T(8,128)(2,1)}, bf16[576,256]{1,0:T(8,128)(2,1)S(1)}, u32[]{:S(2)}, u32[]{:S(2)}) collective-permute-start(bf16[576,256]{1,0:T(8,128)(2,1)} %bitcast.7), channel_id=1, source_target_pairs={{0,2},{1,5},{2,0},{3,7},{4,6},{5,1},{6,4},{7,3},{8,10},{9,13},{10,... | collective-permute-start | bytes 884744 | tf_op jit(solution)/shard_map/ppermute | solution.py:44
  5.1 5.6 %collective-permute-start.3 = (f32[1,16,256]{2,1,0:T(8,128)S(1)}, f32[1,16,256]{2,1,0:T(8,128)S(1)}, u32[]{:S(2)}, u32[]{:S(2)}) collective-permute-start(f32[1,16,256]{2,1,0:T(8,128)S(1)} %bitcast.10), channel_id=1, source_target_pairs={{0,8},{2,10},{4,12},{6,14},{8,0},{10,2},{12,4},{14,6},{1,9},{3,11}... | collective-permute-start | bytes 49160 | tf_op jit(solution)/shard_map/ppermute | solution.py:29
  7.7 5.7 %collective-permute-start.5 = (bf16[80,512]{1,0:T(8,128)(2,1)S(1)}, bf16[80,512]{1,0:T(8,128)(2,1)S(1)}, u32[]{:S(2)}, u32[]{:S(2)}) collective-permute-start(bf16[80,512]{1,0:T(8,128)(2,1)S(1)} %get-tuple-element.11.refs_1_.packed_ref), channel_id=1, source_target_pairs={{0,8},{2,10},{4,12},{6,14},{8,0},{10,2},{12,4},{14,6},{1,9},{3,11}... | collective-permute-start | bytes 245768 | tf_op jit(solution)/shard_map/ppermute | solution.py:29
  8.6 2.1 %collective-permute-start.1 = (bf16[576,256]{1,0:T(8,128)(2,1)S(1)}, bf16[576,256]{1,0:T(8,128)(2,1)S(1)}, u32[]{:S(2)}, u32[]{:S(2)}) collective-permute-start(bf16[576,256]{1,0:T(8,128)(2,1)S(1)} %shard_map.78.first_ref), channel_id=1, source_target_pairs={{0,1},{1,0},{2,3},{3,2},{4,5},{5,4},{6,7},{7,6},{8,9},{9,8},{10,11... | collective-permute-start | bytes 884744 | tf_op jit(solution)/shard_map/ppermute | solution.py:34
  8.6 7.9 %collective-permute-start.2 = (bf16[576,256]{1,0:T(8,128)(2,1)S(1)}, bf16[576,256]{1,0:T(8,128)(2,1)S(1)}, u32[]{:S(2)}, u32[]{:S(2)}) collective-permute-start(bf16[576,256]{1,0:T(8,128)(2,1)S(1)} %shard_map.78.first_ref), channel_id=1, source_target_pairs={{0,4},{1,3},{2,6},{3,1},{4,0},{5,7},{6,2},{7,5},{8,12},{9,11},{10,... | collective-permute-start | bytes 884744 | tf_op jit(solution)/shard_map/ppermute | solution.py:44
  10.7 2.7 %copy-start = (bf16[256,576]{0,1:T(8,128)(2,1)S(1)}, bf16[256,576]{0,1:T(8,128)(2,1)}, u32[]{:S(2)}) copy-start(bf16[256,576]{0,1:T(8,128)(2,1)} %param.7) | copy-start | bytes 884740
  10.7 4.4 %collective-permute-start.4 = (f32[2,16,256]{2,1,0:T(8,128)S(1)}, f32[2,16,256]{2,1,0:T(8,128)S(1)}, u32[]{:S(2)}, u32[]{:S(2)}) collective-permute-start(f32[2,16,256]{2,1,0:T(8,128)S(1)} %shard_map.80.left_ref.refs_1_), channel_id=1, source_target_pairs={{0,2},{2,0},{4,6},{6,4},{8,10},{10,8},{12,14},{14,12},{1,3},{3,1},... | collective-permute-start | bytes 98312 | tf_op jit(solution)/shard_map/ppermute | solution.py:29
  17.0 6.6 %collective-permute-start.6 = (bf16[272,128]{1,0:T(8,128)(2,1)S(1)}, bf16[272,128]{1,0:T(8,128)(2,1)S(1)}, u32[]{:S(2)}, u32[]{:S(2)}) collective-permute-start(bf16[272,128]{1,0:T(8,128)(2,1)S(1)} %shard_map.86), channel_id=1, source_target_pairs={{0,8},{2,10},{4,12},{6,14},{8,0},{10,2},{12,4},{14,6},{1,9},{3,11}... | collective-permute-start | bytes 208904 | tf_op jit(solution)/shard_map/ppermute | solution.py:29
  19.0 4.3 %collective-permute-start.7 = (f32[40,256]{1,0:T(8,128)S(1)}, f32[40,256]{1,0:T(8,128)S(1)}, u32[]{:S(2)}, u32[]{:S(2)}) collective-permute-start(f32[40,256]{1,0:T(8,128)S(1)} %shard_map.81.refs_1_), channel_id=1, source_target_pairs={{0,4},{2,6},{4,0},{6,2},{8,12},{10,14},{12,8},{14,10},{1,5},{3,7},... | collective-permute-start | bytes 122888 | tf_op jit(solution)/shard_map/ppermute | solution.py:29
